TPU v7x, 256 devices: a whole 4x4x8 slice. The times are simulated.
256 devices in a mesh: enc: 32 (over z_lo, x, core), tp: 8 (over z_hi, y).
Axes of the slice: x: 4, y: 4, z: 8 (z_hi: 2, z_lo: 4; z = z_hi * 4 + z_lo), core: 2. Of those that a mesh axis runs over, the one named last changes fastest.
Arguments:
- vit_hidden: bfloat16 [2, 14336, 4608], P(None, ('enc', 'tp')), may hold values from -6 to 6
- merge_weight: bfloat16 [2, 4608, 5120], P(None, 'enc', 'tp'), may hold values from -0.09375 to 0.09375
- merge_bias: bfloat16 [2, 5120], P(None, 'tp'), may hold values from -3 to 3
- residual: bfloat16 [2, 65536, 5120], P(None, ('enc', 'tp')), may hold values from -6 to 6
- norm_gain: bfloat16 [2, 5120], replicated, may hold values from 0.5 to 1.5
- image_sequence: int32 [896], P('enc'), may hold values from 0 to 31, as said below
- token_source: int32 [65536], P('enc'), may hold values from -1 to 1023, as said below
Outputs:
- normed: bfloat16 [2, 65536, 5120], P(None, ('enc', 'tp'))
Inputs may be any that keep to these rules, and one draw needn't show every extreme that they name: `image_sequence`: each encoder shard assigns at most 2 images to one sequence, and exactly 2 to some sequence in every draw; every sequence receives exactly 28 images. `token_source`: consistent with image_sequence: every image's 16 rows appear once, at 16 consecutive tokens of its own sequence, in row order; images do not intersect; all other tokens are -1.
All inputs are finite; a program needn't handle non-finite values.
Results may differ from a plain program's by a relative error of at most 0.0036.
Values may be sent and summed in bfloat16 or wider, within the bound.
A program may use at most 128 MiB of HBM per device.

v0:
```python
import jax
import jax.numpy as jnp
from jax import lax
from jax.sharding import PartitionSpec as P

IMG = 16
CAP = 2


def source_rank(destinations):
    count = destinations.shape[0]
    same = destinations[:, None] == destinations[None, :]
    order = jnp.arange(count, dtype=jnp.int32)
    earlier = order[None, :] < order[:, None]
    return jnp.sum(jnp.logical_and(same, earlier), axis=1)


def pack_slots(rows, destinations, ranks, shards):
    count = destinations.shape[0]
    width = rows.shape[-1]
    grouped = rows.reshape(count, IMG, width)
    slots = jnp.zeros((shards, CAP, IMG, width), rows.dtype)
    slots = slots.at[destinations, ranks].set(grouped)
    return slots.reshape(shards, CAP * IMG, width)


def place_tokens(arrived, sources):
    flat = arrived.reshape(-1, arrived.shape[-1])
    padded = jnp.concatenate([flat, jnp.zeros((1, flat.shape[1]), flat.dtype)], axis=0)
    index = jnp.where(sources < 0, flat.shape[0], sources)
    return jnp.take(padded, index, axis=0)


def inject(stream, deep, gain):
    updated = (stream.astype(jnp.float32) + deep.astype(jnp.float32)).astype(jnp.bfloat16)
    values = lax.optimization_barrier(updated).astype(jnp.float32)
    scale = lax.rsqrt(jnp.mean(values * values, axis=-1, keepdims=True) + 1e-06)
    return (values * scale * gain.astype(jnp.float32)).astype(jnp.bfloat16)


def per_device(
    vit_hidden, merge_weight, merge_bias, residual, norm_gain, image_sequence, token_source
):
    shards = lax.axis_size("enc")
    levels = vit_hidden.shape[0]
    width = merge_weight.shape[2]
    ranks = source_rank(image_sequence)
    results = []
    for level in range(levels):
        gathered = lax.all_gather(vit_hidden[level], "tp", axis=0, tiled=True)

        def accumulate(total, piece, start, gathered=gathered):
            return jnp.dot(gathered, piece, preferred_element_type=jnp.float32)

        empty = jnp.zeros((gathered.shape[0], width), jnp.float32)
        projected = accumulate(
            empty, lax.all_gather(merge_weight[level], "enc", axis=0, tiled=True), jnp.int32(0)
        )
        merged = (projected + merge_bias[level].astype(jnp.float32)).astype(jnp.bfloat16)
        outgoing = pack_slots(merged, image_sequence, ranks, shards)
        arrived = lax.all_to_all(outgoing, "enc", split_axis=0, concat_axis=0, tiled=True)
        sequence_rows = place_tokens(arrived, token_source)
        deep = lax.all_to_all(sequence_rows, "tp", split_axis=0, concat_axis=1, tiled=True)
        results.append(inject(residual[level], deep, norm_gain[level]))
    return jnp.stack(results)


def solution(mesh):
    return jax.shard_map(
        per_device,
        mesh=mesh,
        in_specs=(
            P(None, ("enc", "tp"), None),
            P(None, "enc", "tp"),
            P(None, "tp"),
            P(None, ("enc", "tp"), None),
            P(),
            P("enc"),
            P("enc"),
        ),
        out_specs=P(None, ("enc", "tp"), None),
        check_vma=False,
    )
```

profile of v0, /device:TPU:32, one launch (start us, length us, event | category | flops | bytes accessed | tf_op | source)
XLA Modules:
  0.0 574.5 jit_solution(7549177765676171371)
XLA Ops:
  6.5 2.3 fusion.41
  8.9 0.8 fusion.42
  9.8 0.7 all-gather.13.cloned.1.call-update
  10.5 0.5 all-gather.15.cloned.1.call-update
  11.3 106.4 %all-gather.9.cloned.1.call-done = bf16[1,448,4608]{2,1,0:T(8,128)(2,1)} async-done(((bf16[1,56,4608]{2,1,0:T(8,128)(2,1)}), bf16[1,448,4608]{2,1,0:T(8,128)(2,1)}) %all-gather.9.cloned.1.call-update) | async-done | bytes 4128784 | tf_op jit(solution)/shard_map/all_gather | solution.py:50
  117.7 63.1 %all-gather.11.cloned.1.call-done = bf16[1,4608,640]{2,1,0:T(8,128)(2,1)} async-done(((bf16[1,144,640]{2,1,0:T(8,128)(2,1)}), bf16[1,4608,640]{2,1,0:T(8,128)(2,1)}) %all-gather.11.cloned.1.call-update) | async-done | bytes 5898256 | tf_op jit(solution)/shard_map/all_gather | solution.py:57
  180.8 7.3 %fusion.31 = bf16[448,640]{1,0:T(8,128)(2,1)S(1)} fusion(bf16[1,4608,640]{2,1,0:T(8,128)(2,1)} %all-gather.11.cloned.1.call-done, bf16[1,448,4608]{2,1,0:T(8,128)(2,1)} %all-gather.9.cloned.1.call-done, f32[640]{0:T(1024)S(1)} %get-tuple-element.6), kind=kOutput, calls=%fused_computation.34 | convolution fusion | flops 2642984960 | bytes 10603008 | tf_op jit(solution)/shard_map/dot_general | solution.py:53
  188.1 1.2 broadcast.69.clone
  189.2 4.7 scatter_fusion
  193.9 5.9 %all-to-all-start = ((bf16[32,32,640]{2,1,0:T(8,128)(2,1)}), bf16[32,32,640]{2,1,0:T(8,128)(2,1)S(1)}, u32[]{:S(2)}, u32[]{:S(2)}) async-start(bf16[32,32,640]{2,1,0:T(8,128)(2,1)} %bitcast.7), calls=%async_computation | async-start | bytes 2621440 | tf_op jit(solution)/shard_map/all_to_all | solution.py:61
  199.9 97.4 %all-gather.13.cloned.1.call-done = bf16[1,448,4608]{2,1,0:T(8,128)(2,1)} async-done(((bf16[1,56,4608]{2,1,0:T(8,128)(2,1)}), bf16[1,448,4608]{2,1,0:T(8,128)(2,1)}) %all-gather.13.cloned.1.call-update) | async-done | bytes 4128784 | tf_op jit(solution)/shard_map/all_gather | solution.py:50
  297.3 63.7 %all-gather.15.cloned.1.call-done = bf16[1,4608,640]{2,1,0:T(8,128)(2,1)} async-done(((bf16[1,144,640]{2,1,0:T(8,128)(2,1)}), bf16[1,4608,640]{2,1,0:T(8,128)(2,1)}) %all-gather.15.cloned.1.call-update) | async-done | bytes 5898256 | tf_op jit(solution)/shard_map/all_gather | solution.py:57
  361.0 7.3 %fusion.26 = bf16[448,640]{1,0:T(8,128)(2,1)S(1)} fusion(bf16[1,4608,640]{2,1,0:T(8,128)(2,1)} %all-gather.15.cloned.1.call-done, bf16[1,448,4608]{2,1,0:T(8,128)(2,1)} %all-gather.13.cloned.1.call-done, f32[640]{0:T(1024)S(1)} %get-tuple-element.7), kind=kOutput, calls=%fused_computation.33 | convolution fusion | flops 2642984960 | bytes 10603008 | tf_op jit(solution)/shard_map/dot_general | solution.py:53
  368.3 1.2 broadcast.69.clone.1
  369.4 4.7 scatter_fusion.1
  374.2 6.2 %all-to-all-start.2 = ((bf16[32,32,640]{2,1,0:T(8,128)(2,1)}), bf16[32,32,640]{2,1,0:T(8,128)(2,1)}, u32[]{:S(2)}, u32[]{:S(2)}) async-start(bf16[32,32,640]{2,1,0:T(8,128)(2,1)} %bitcast.17), calls=%async_computation.2 | async-start | bytes 2621440 | tf_op jit(solution)/shard_map/all_to_all | solution.py:61
  380.5 9.3 %gather_fusion = bf16[2048,640]{1,0:T(8,128)(2,1)} fusion(bf16[1025,640]{1,0:T(8,128)(2,1)S(1)} %concatenate.11, s32[2048]{0:T(1024)S(1)} %fusion.37), kind=kCustom, calls=%fused_computation.clone | custom fusion | bytes 5251072 | tf_op jit(solution)/shard_map/jit(_take)/gather | solution.py:31
  389.8 21.2 %all-to-all-done.2 = bf16[32,32,640]{2,1,0:T(8,128)(2,1)} async-done(((bf16[32,32,640]{2,1,0:T(8,128)(2,1)}), bf16[32,32,640]{2,1,0:T(8,128)(2,1)}, u32[]{:S(2)}, u32[]{:S(2)}) %all-to-all-start.2) | async-done | bytes 1310752 | tf_op jit(solution)/shard_map/all_to_all | solution.py:61
  411.0 1.4 concatenate.12
  412.4 9.3 %gather_fusion.1 = bf16[2048,640]{1,0:T(8,128)(2,1)} fusion(bf16[1025,640]{1,0:T(8,128)(2,1)S(1)} %concatenate.12, s32[2048]{0:T(1024)S(1)} %fusion.37), kind=kCustom, calls=%fused_computation.1.clone | custom fusion | bytes 5251072 | tf_op jit(solution)/shard_map/jit(_take)/gather | solution.py:31
  421.7 3.9 broadcast_select_fusion.1
  425.7 72.8 %all_to_all.36 = bf16[8,256,640]{2,1,0:T(8,128)(2,1)} all-to-all(bf16[8,256,640]{2,1,0:T(8,128)(2,1)S(1)} %bitcast.70), channel_id=1, replica_groups=mesh['enc'=32,'tp'=8] {'tp'}, dimensions={0} | all-to-all | bytes 5242880 | tf_op jit(solution)/shard_map/all_to_all | solution.py:63
  498.5 3.9 all-to-all-start.3
  502.5 2.1 convert_bitcast_fusion.1
  504.6 3.0 copy.12
  507.6 43.8 %all-to-all-done.3 = bf16[8,256,640]{2,1,0:T(8,128)(2,1)S(1)} async-done(((bf16[8,256,640]{2,1,0:T(8,128)(2,1)}), bf16[8,256,640]{2,1,0:T(8,128)(2,1)S(1)}, u32[]{:S(2)}, u32[]{:S(2)}) %all-to-all-start.3) | async-done | bytes 2621472 | tf_op jit(solution)/shard_map/all_to_all | solution.py:63
  551.8 2.9 copy.13
  554.7 7.2 %fusion.11 = (bf16[256,5120]{1,0:T(8,128)(2,1)S(1)}, bf16[256,5120]{1,0:T(8,128)(2,1)S(1)}) fusion(f32[256,5120]{1,0:T(8,128)} %bitcast.68, bf16[2,256,5120]{2,1,0:T(8,128)(2,1)} %param.12, f32[256,5120]{1,0:T(8,128)} %bitcast.69), kind=kLoop, calls=%fused_computation.22 | loop fusion | flops 7864320 | bytes 20971520 | tf_op jit(solution)/shard_map/convert_element_type | solution.py:35
  561.9 0.6 fusion.7
  562.5 0.6 fusion.4
  563.1 2.0 fusion.14
  565.2 2.8 pad_maximum_fusion
  (27 shorter events, 0.9 us)
Async XLA Ops:
  6.5 2.4 copy-start
  6.5 4.5 copy-start.3
  6.5 4.5 copy-start.4
  6.5 111.2 %all-gather.9.cloned.1.call-start = ((), (), s32[]{:S(2)}) async-start(), calls=%async_computation.4 | async-start | bytes 4644864 | tf_op jit(solution)/shard_map/all_gather | solution.py:50
  8.8 171.9 %all-gather.11.cloned.1.call-start = ((), (), s32[]{:S(2)}) async-start(), calls=%async_computation.5 | async-start | bytes 6082560 | tf_op jit(solution)/shard_map/all_gather | solution.py:57
  9.7 287.6 %all-gather.13.cloned.1.call-start = ((), (), s32[]{:S(2)}) async-start(), calls=%async_computation.6 | async-start | bytes 4644864 | tf_op jit(solution)/shard_map/all_gather | solution.py:50
  10.5 350.5 %all-gather.15.cloned.1.call-start = ((), (), s32[]{:S(2)}) async-start(), calls=%async_computation.7 | async-start | bytes 6082560 | tf_op jit(solution)/shard_map/all_gather | solution.py:57
  193.9 180.2 %all-to-all-start = ((bf16[32,32,640]{2,1,0:T(8,128)(2,1)}), bf16[32,32,640]{2,1,0:T(8,128)(2,1)S(1)}, u32[]{:S(2)}, u32[]{:S(2)}) async-start(bf16[32,32,640]{2,1,0:T(8,128)(2,1)} %bitcast.7), calls=%async_computation | async-start | bytes 2621440 | tf_op jit(solution)/shard_map/all_to_all | solution.py:61
  368.3 12.0 %copy-start.2 = (s32[2048]{0:T(1024)S(1)}, s32[2048]{0:T(1024)}, u32[]{:S(2)}) copy-start(s32[2048]{0:T(1024)} %param.15) | copy-start | bytes 24580
  374.2 36.8 %all-to-all-start.2 = ((bf16[32,32,640]{2,1,0:T(8,128)(2,1)}), bf16[32,32,640]{2,1,0:T(8,128)(2,1)}, u32[]{:S(2)}, u32[]{:S(2)}) async-start(bf16[32,32,640]{2,1,0:T(8,128)(2,1)} %bitcast.17), calls=%async_computation.2 | async-start | bytes 2621440 | tf_op jit(solution)/shard_map/all_to_all | solution.py:61
  498.5 4.0 copy-start.1
  498.5 52.9 %all-to-all-start.3 = ((bf16[8,256,640]{2,1,0:T(8,128)(2,1)}), bf16[8,256,640]{2,1,0:T(8,128)(2,1)S(1)}, u32[]{:S(2)}, u32[]{:S(2)}) async-start(bf16[8,256,640]{2,1,0:T(8,128)(2,1)} %bitcast.19), calls=%async_computation.3 | async-start | bytes 5242880 | tf_op jit(solution)/shard_map/all_to_all | solution.py:63
Sparse Core Ops, SparseCore 0:
  10.0 107.6 all-gather.8
  119.6 61.1 all-gather.10
  183.4 113.8 all-gather.12
  299.0 61.9 all-gather.14
where the time goes:
time: 578 us; the launch traced here: 575 us
  waiting for transfers between devices  397 us (69%)
  blocking collectives  72.8 us (13%)
  local copies, waits for them, and re-layouts  40.9 us (7%)
  other arithmetic  19.9 us (3%)
  starting transfers between devices  16.1 us (3%)
  matrix products  14.6 us (3%)
  between operations  13.3 us (2%)
    all_gather x2, waiting for transfers between devices, per_device(): gathered = lax.all_gather(vit_hidden[level], 'tp', axis=0, tiled=True)  204 us
    all_gather x2, waiting for transfers between devices, per_device(): lax.all_gather(merge_weight[level], 'enc', axis=0, tiled=True)  127 us
    all_to_all x1, blocking collectives, per_device(): lax.all_to_all(sequence_rows, 'tp', split_axis=0, concat_axis=1, tiled=True)  72.8 us
    all_to_all x1, waiting for transfers between devices, per_device(): lax.all_to_all(sequence_rows, 'tp', split_axis=0, concat_axis=1, tiled=True)  43.8 us
    all_to_all x2, waiting for transfers between devices, per_device(): lax.all_to_all(outgoing, 'enc', split_axis=0, concat_axis=0, tiled=True)  21.2 us
    gather x2, local copies, waits for them, and re-layouts, place_tokens(): return jnp.take(padded, index, axis=0)  18.7 us
    dot_general x2, matrix products, accumulate(): return jnp.dot(gathered, piece, preferred_element_type=jnp.float32)  14.6 us
    all_to_all x2, starting transfers between devices, per_device(): lax.all_to_all(outgoing, 'enc', split_axis=0, concat_axis=0, tiled=True)  12.1 us
  transfers between devices with their start and end apart: 7, of which 6 were waited for; matrix products, arithmetic and copies ran while one was open for 7% of the time, Pallas kernels for 0%

commit v1 on v0

v1 whole, which is shorter than its diff:
```python
import functools

import jax
import jax.numpy as jnp
from jax import lax
from jax.experimental import pallas as pl
from jax.experimental.pallas import tpu as pltpu
from jax.sharding import PartitionSpec as P

MESH = pl.DeviceIdType.MESH
BF16, F32, I32 = jnp.bfloat16, jnp.float32, jnp.int32

IMG = 16
WIN = 17
ROWS = 56
IMGS = 14
HALF = IMGS * IMG
K = 4608
TILE = 128
UNITS = 5
SENDS = 160


def place(enc, tp):
    z_lo, rest = lax.div(enc, 8), lax.rem(enc, 8)
    return z_lo, lax.div(rest, 2), lax.rem(rest, 2), lax.div(tp, 4), lax.rem(tp, 4)


def device(z_lo, x, core, z_hi, y):
    return (z_lo * 8 + x * 2 + core, z_hi * 4 + y)


def running(values):
    count = values.shape[0]
    row = lax.broadcasted_iota(I32, values.shape, 0)
    total = values
    step = 1
    while step < count:
        total = total + jnp.where(row >= step, pltpu.roll(total, step, 0), 0)
        step *= 2
    return total - values


def exchange(
    vit, w, bias, seq, tokens,
    arrived, keys,
    held, weight, g0, g1, g2, g3, g4, staged, acc, joined, other_bias, table, lists, list_s,
    ssem, rsem, lsem, ws, wr, ls, lr, ds, dr,
):
    gathered = (g0, g1, g2, g3, g4)
    enc, tp = lax.axis_index("enc"), lax.axis_index("tp")
    z_lo, x, core, z_hi, y = place(enc, tp)
    z = z_hi * 4 + z_lo
    odd = lax.rem(x, 2)
    x_half = lax.div(x, 2)

    def at_xy(dx, dy):
        return device(z_lo, lax.rem(x + dx + 4, 4), core, z_hi, lax.rem(y + dy + 4, 4))

    def at_z(d):
        there = lax.rem(z + d + 8, 8)
        return device(lax.rem(there, 4), x, core, lax.div(there, 4), y)

    sibling = device(z_lo, x, 1 - core, z_hi, y)
    across = device(z_lo, x, core, 1 - z_hi, y)

    def at_lo(d):
        return device(lax.rem(z_lo + d, 4), x, core, z_hi, y)

    def scatter_to(b):
        return device(z_lo, 2 * z_hi + b, core, x_half, y)

    far = x_half != z_hi

    barrier = pltpu.get_barrier_semaphore()
    peers = [at_xy(d // 4, d % 4) for d in range(1, 16)]
    peers += [at_z(1), at_z(-1), sibling, across] + [at_lo(d) for d in (1, 2, 3)]
    for peer in peers:
        pl.semaphore_signal(barrier, inc=1, device_id=peer, device_id_type=MESH)

    @pl.when(far)
    def _():
        for b in range(2):
            pl.semaphore_signal(barrier, inc=1, device_id=scatter_to(b), device_id_type=MESH)

    pl.semaphore_wait(barrier, len(peers) + jnp.where(far, 2, 0))

    sends = []

    def put(src, dst, to):
        number = len(sends)
        copy = pltpu.make_async_remote_copy(
            src_ref=src, dst_ref=dst, send_sem=ssem.at[number], recv_sem=rsem.at[number],
            device_id=to, device_id_type=MESH,
        )
        copy.start()
        sends.append(copy)
        return number

    def got(number, dst):
        pltpu.make_async_remote_copy(
            src_ref=dst, dst_ref=dst, send_sem=ssem.at[number], recv_sem=rsem.at[number],
            device_id=sibling, device_id_type=MESH,
        ).wait_recv()

    part = K // 2

    def block(level, p, rx, ry, half=None):
        rows = pl.ds(0, 64) if level == 0 else pl.ds(64, 48)
        if half is None:
            return held.at[rx * 4 + ry, rows, pl.ds(p * part, part)]
        return held.at[rx * 4 + ry, rows, pl.ds(p * part + half * (part // 2), part // 2)]

    def near(p, first, second):
        return (second, first) if p == 0 else (first, second)

    def step_to(p, axis, d):
        return at_xy(*(near(p, d, 0) if axis == 0 else near(p, 0, d)))

    ids = {}

    def send_block(level, p, axis, d, first, second, half=None, src=None):
        if axis == 0:
            there = ((first - d) % 4, second)
        else:
            there = (first, (second - d) % 4)
        src = block(level, p, *near(p, first, second), half) if src is None else src
        ids[(level, p, there, half)] = put(
            src, block(level, p, *near(p, *there), half), step_to(p, axis, d)
        )

    def have(level, p, first, second, half=None):
        got(ids[(level, p, (first, second), half)], block(level, p, *near(p, first, second), half))

    def vit_own(level):
        rows = pl.ds(0, 64) if level == 0 else pl.ds(64, 48)
        for axis in range(2):
            for p in range(2):
                for d in (1, -1):
                    send_block(level, p, axis, d, 0, 0, src=vit.at[rows, pl.ds(p * part, part)])

    def vit_step(level, number):
        both = (0, 1)
        if number == 1:
            for p in both:
                for d in (1, -1):
                    off = (-d) % 4
                    have(level, p, off, 0)
                    send_block(level, p, 0, d, off, 0, half=0 if d == 1 else 1)
                    for d2 in (1, -1):
                        send_block(level, p, 1, d2, off, 0)
        if number == 2:
            for p in both:
                for d in (1, -1):
                    off = (-d) % 4
                    have(level, p, 0, off)
                    send_block(level, p, 1, d, 0, off, half=0 if d == 1 else 1)
        if number == 3:
            for p in both:
                for half in both:
                    have(level, p, 2, 0, half)
                for d2 in (1, -1):
                    send_block(level, p, 1, d2, 2, 0)
        if number == 4:
            for first in (3, 1):
                for p in both:
                    for d in (1, -1):
                        off = (-d) % 4
                        have(level, p, first, off)
                        send_block(level, p, 1, d, first, off, half=0 if d == 1 else 1)
        if number == 5:
            for p in both:
                for d in (1, -1):
                    off = (-d) % 4
                    have(level, p, 2, off)
                    send_block(level, p, 1, d, 2, off, half=0 if d == 1 else 1)
        if number == 6:
            for first in (0, 3, 1, 2):
                for p in both:
                    for half in both:
                        have(level, p, first, 2, half)

    def scatter_parts(b):
        mine = weight.at[z_lo * 2 + x_half, odd, core]
        return (
            (w.at[0, :, pl.ds(384 * b, 256)], mine.at[:, pl.ds(0, 256)]),
            (w.at[b, :, pl.ds(256, 128)], mine.at[:, pl.ds(256, 128)]),
            (w.at[1, :, pl.ds(384 * b, 256)], mine.at[:, pl.ds(384, 256)]),
        )

    def scatter_copy(b, i):
        src, dst = scatter_parts(b)[i]
        return pltpu.make_async_remote_copy(
            src_ref=src, dst_ref=dst, send_sem=ws.at[b, i], recv_sem=wr.at[odd, i],
            device_id=scatter_to(b), device_id_type=MESH,
        )

    def stays(b):
        return jnp.logical_and(2 * z_hi + b == x, jnp.logical_not(far))

    def weight_scatter():
        for b in range(2):
            @pl.when(stays(b))
            def _():
                for i, (src, dst) in enumerate(scatter_parts(b)):
                    pltpu.make_async_copy(src, dst, wr.at[odd, i]).start()

            @pl.when(jnp.logical_not(stays(b)))
            def _():
                for i in range(3):
                    scatter_copy(b, i).start()

    def rows_of(d, whose=None):
        there = lax.rem(z + d + 8, 8)
        index = lax.rem(there, 4) * 2 + lax.div(there, 4)
        return weight.at[index, :, core if whose is None else whose]

    wid = {}

    def ring_send(kind, store, view, d, up):
        to = at_z(1) if up else at_z(-1)
        there = d - 1 if up else d + 1
        if abs(there) == 4:
            piece = view(d, 0 if up else 1)
        else:
            piece = view(d, None)
        store[(kind, there)] = put(piece, piece, to)

    def weight_view(d, half):
        there = lax.rem(z + d + 8, 8)
        index = lax.rem(there, 4) * 2 + lax.div(there, 4)
        if half is None:
            return weight.at[index, :, core]
        return weight.at[index, half, core]

    def weight_step(number):
        if number == 0:
            for i in range(2):
                for k, cols in enumerate(((0, 256), (256, 128), (384, 256))):
                    landing = weight.at[z_lo * 2 + z_hi, i, core, :, pl.ds(*cols)]
                    pltpu.make_async_remote_copy(
                        src_ref=landing, dst_ref=landing, send_sem=ws.at[0, k], recv_sem=wr.at[i, k],
                        device_id=sibling, device_id_type=MESH,
                    ).wait_recv()
            for up in (True, False):
                ring_send("w", wid, weight_view, 0, up)
            wid[("s", 0)] = put(weight_view(0, None), weight_view(0, None), sibling)
        else:
            ring_step("w", wid, weight_view, number)
            if number == 4:
                for d in (0, -1, 1, -2, 2, -3, 3, 4):
                    got(wid[("s", d)], rows_of(d, 1 - core))

    def ring_step(kind, store, view, number):
        if number < 4:
            for d, up in ((-number, True), (number, False)):
                got(store[(kind, d)], view(d, None))
                ring_send(kind, store, view, d, up)
                store[("s", d)] = put(view(d, None), view(d, None), sibling)
        else:
            got(store[(kind, -4)], view(-4, 0))
            got(store[(kind, 4)], view(4, 1))
            store[("s", 4)] = put(view(4, None), view(4, None), sibling)

    def merged_view(g, d, half, whose):
        start = (whose * 8 + lax.rem(z + d + 8, 8)) * (4 * IMGS)
        if half is None:
            return g.at[pl.ds(start, 4 * IMGS)]
        return g.at[pl.ds(start + half * 2 * IMGS, 2 * IMGS)]

    gid = [dict() for _ in range(UNITS)]

    def unit_view(unit):
        return lambda d, half: merged_view(gathered[unit], d, half, core)

    def unit_step(unit, number):
        view = unit_view(unit)
        if number == 0:
            for up in (True, False):
                ring_send("g", gid[unit], view, 0, up)
            gid[unit][("s", 0)] = put(view(0, None), view(0, None), sibling)
        elif number < 5:
            ring_step("g", gid[unit], view, number)
        else:
            for d in (0, -1, 1, -2, 2, -3, 3, 4):
                got(gid[unit][("s", d)], merged_view(gathered[unit], d, None, 1 - core))

    def project(level, column, width, units, bias_row):
        def one(r, _):
            def chunk(k, _):
                rows = held[pl.ds(r * 4, 4), pl.ds(pl.multiple_of(level * 48, 16), 64),
                            pl.ds(pl.multiple_of(k * part, TILE), part)]
                cols = weight[pl.ds(k * 4, 4), :, :, :, column:column + width]
                product = jnp.dot(
                    rows.reshape(256, part), cols.reshape(part, width), preferred_element_type=F32
                )

                @pl.when(k == 0)
                def _():
                    acc[:, :width] = product

                @pl.when(k != 0)
                def _():
                    acc[:, :width] += product
                return 0

            lax.fori_loop(0, 2, chunk, 0)
            for ry in range(4):
                start = pl.multiple_of(lax.rem(y + ry, 4) * ROWS, 8)
                joined[pl.ds(start, ROWS), :width] = acc[
                    pl.ds(pl.multiple_of(ry * 64 + level * 8, 8), ROWS), :width
                ]
            start = ((core * 8 + z) * 4 + lax.rem(x + r, 4)) * IMGS
            for i, unit in enumerate(units):
                cols = slice(i * TILE, (i + 1) * TILE)
                gathered[unit][pl.ds(start, IMGS)] = (
                    joined[:, cols] + bias_row[:, cols]
                ).astype(BF16).reshape(IMGS, IMG, TILE)
            return 0

        lax.fori_loop(0, 4, one, 0)

    def bias_of(level, column, width):
        mine = jnp.where(far, other_bias[...], bias[...])
        row = jnp.where(level == 0, mine[0:1], mine[1:2])
        if column is None:
            return jnp.where(odd == 0, row[:, 0:width], row[:, 384:384 + width])
        return row[:, column:column + width]

    def window_send(unit):
        g = gathered[unit]

        def one(d, _):
            dx, dy = lax.div(d, 4), lax.rem(d, 4)
            there = lax.rem(x + dx, 4) * 4 + lax.rem(y + dy, 4)
            for k in range(WIN):
                staged[unit, d, k] = g[list_s[there, 0, k]]
            dst = arrived.at[x * 4 + y, :, :, pl.ds(unit * TILE, TILE)]

            @pl.when(d == 0)
            def _():
                pltpu.make_async_copy(staged.at[unit, d], dst, dr.at[unit, d]).start()

            @pl.when(d != 0)
            def _():
                pltpu.make_async_remote_copy(
                    src_ref=staged.at[unit, d], dst_ref=dst, send_sem=ds.at[unit, d], recv_sem=dr.at[unit, d],
                    device_id=at_xy(dx, dy), device_id_type=MESH,
                ).start()
            return 0

        lax.fori_loop(0, 16, one, 0)

    def window_wait(unit):
        dst0 = arrived.at[x * 4 + y, :, :, pl.ds(unit * TILE, TILE)]
        pltpu.make_async_copy(staged.at[unit, 0], dst0, dr.at[unit, 0]).wait()

        def one(d, _):
            dx, dy = lax.div(d, 4), lax.rem(d, 4)
            here = lax.rem(x - dx + 4, 4) * 4 + lax.rem(y - dy + 4, 4)
            copy = pltpu.make_async_remote_copy(
                src_ref=staged.at[unit, d], dst_ref=arrived.at[here, :, :, pl.ds(unit * TILE, TILE)],
                send_sem=ds.at[unit, d], recv_sem=dr.at[unit, d],
                device_id=at_xy(dx, dy), device_id_type=MESH,
            )
            copy.wait_send()
            copy.wait_recv()
            return 0

        lax.fori_loop(1, 16, one, 0)

    lane = lax.broadcasted_iota(I32, (32, 128), 1)
    sub = lax.broadcasted_iota(I32, (32, 128), 0)

    def own_table():
        ours = jnp.where(seq[...] == lax.div(lane, 2), 1, 0)
        second = jnp.where(sub >= 14, 1, 0)
        where = ((core * 8 + second * 4 + z_lo) * 4 + x) * 14 + sub - 14 * second
        pick = jnp.logical_and(ours == 1, running(ours) == lax.rem(lane, 2))
        row = jnp.sum(jnp.where(pick, where, 0), axis=0, keepdims=True)
        table[enc] = jnp.broadcast_to(row, (8, 128))

    def own_list():
        here = [tokens[pl.ds(tp * 2 + i, 1), :] for i in range(2)]
        slots = [lax.shift_right_arithmetic(row, 4) for row in here]
        total = jnp.zeros((1, 128), I32)
        picked = jnp.zeros((1, 128), I32)
        key = [jnp.zeros((1, 128), I32) for _ in range(2)]
        for rank in range(2):
            hit = [jnp.where(row == sub * 2 + rank, 1, 0) for row in slots]
            present = jnp.max(jnp.maximum(hit[0], hit[1]), axis=1, keepdims=True)
            present = jnp.broadcast_to(present, (32, 128))
            position = running(present) + total
            total = total + jnp.sum(present, axis=0, keepdims=True)
            places = jnp.where(lane == enc * 2 + rank, table[:, 0, :], 0)
            places = jnp.sum(places, axis=1, keepdims=True)
            chosen = jnp.logical_and(present == 1, position == lane)
            picked = picked + jnp.sum(jnp.where(chosen, places, 0), axis=0, keepdims=True)
            for i in range(2):
                key[i] = key[i] + jnp.sum(hit[i] * position, axis=0, keepdims=True)
        lists[x * 4 + y] = jnp.broadcast_to(picked, (8, 128))
        for i in range(2):
            keys[i:i + 1, :] = jnp.where(here[i] < 0, -1, key[i] * IMG + jnp.bitwise_and(here[i], IMG - 1))

    def list_copy(d, back):
        dx, dy = lax.div(d, 4), lax.rem(d, 4)
        sign = -1 if back else 1
        slot = lax.rem(x - dx + 4, 4) * 4 + lax.rem(y - dy + 4, 4) if back else x * 4 + y
        return pltpu.make_async_remote_copy(
            src_ref=lists.at[x * 4 + y], dst_ref=lists.at[slot], send_sem=ls.at[d], recv_sem=lr.at[d],
            device_id=at_xy(dx, dy), device_id_type=MESH,
        )

    def list_send():
        def one(d, _):
            list_copy(d, False).start()
            return 0
        lax.fori_loop(1, 16, one, 0)

    def list_wait():
        def one(d, _):
            copy = list_copy(d, True)
            copy.wait_send()
            copy.wait_recv()
            return 0
        lax.fori_loop(1, 16, one, 0)
        copy = pltpu.make_async_copy(lists, list_s, lsem.at[1])
        copy.start()
        copy.wait()

    vit_own(0)
    mine = pltpu.make_async_copy(vit, held.at[0], lsem.at[0])
    mine.start()
    weight_scatter()
    bias_id = put(bias, other_bias, across)
    own_table()
    own = table.at[enc]
    sib_id = put(own, own, sibling)
    vit_step(0, 1)
    weight_step(0)
    got(sib_id, table.at[z_lo * 8 + x * 2 + 1 - core])
    pair = table.at[pl.ds(z_lo * 8 + x * 2, 2)]
    pair_ids = [put(pair, pair, at_xy(d, 0)) for d in (1, 2, 3)]
    vit_step(0, 2)
    for d, number in zip((1, 2, 3), pair_ids):
        got(number, table.at[pl.ds(z_lo * 8 + lax.rem(x - d + 4, 4) * 2, 2)])
    eight = table.at[pl.ds(z_lo * 8, 8)]
    lo_ids = [put(eight, eight, at_lo(d)) for d in (1, 2, 3)]
    weight_step(1)
    vit_step(0, 3)
    for d, number in zip((1, 2, 3), lo_ids):
        got(number, table.at[pl.ds(lax.rem(z_lo - d + 4, 4) * 8, 8)])
    own_list()
    list_send()
    weight_step(2)
    vit_step(0, 4)
    vit_own(1)
    weight_step(3)
    vit_step(0, 5)
    list_wait()
    got(bias_id, other_bias)
    weight_step(4)
    mine.wait()
    vit_step(0, 6)
    project(0, 0, 256, (0, 1), bias_of(0, None, 256))
    unit_step(0, 0)
    unit_step(1, 0)
    vit_step(1, 1)
    unit_step(0, 1)
    vit_step(1, 2)
    unit_step(1, 1)
    vit_step(1, 3)
    unit_step(0, 2)
    vit_step(1, 4)
    unit_step(1, 2)
    vit_step(1, 5)
    unit_step(0, 3)
    unit_step(1, 3)
    vit_step(1, 6)
    project(odd, 256, 128, (2,), bias_of(odd, 256, 128))
    unit_step(2, 0)
    project(1, 384, 256, (3, 4), bias_of(1, None, 256))
    unit_step(3, 0)
    unit_step(0, 4)
    unit_step(1, 4)
    unit_step(0, 5)
    unit_step(2, 1)
    window_send(0)
    unit_step(3, 1)
    unit_step(2, 2)
    unit_step(1, 5)
    window_send(1)
    unit_step(3, 2)
    unit_step(4, 0)
    unit_step(2, 3)
    unit_step(3, 3)
    unit_step(4, 1)
    unit_step(2, 4)
    unit_step(3, 4)
    unit_step(4, 2)
    unit_step(2, 5)
    window_send(2)
    unit_step(3, 5)
    window_send(3)
    unit_step(4, 3)
    unit_step(4, 4)
    unit_step(4, 5)
    window_send(4)
    for unit in range(UNITS):
        window_wait(unit)
    for copy in sends:
        copy.wait_send()
    for b in range(2):
        @pl.when(jnp.logical_not(stays(b)))
        def _():
            for i in range(3):
                scatter_copy(b, i).wait_send()


def finish(keys, arrived, residual, gain, out):
    level = pl.program_id(0)
    tokens = residual.shape[1]
    key = jnp.concatenate([keys[0:1, :], keys[1:2, :]], axis=1)
    hot = jnp.where(lax.broadcasted_iota(I32, (WIN * IMG, tokens), 0) == key, 1.0, 0.0).astype(BF16)

    def for_level(lvl):
        square = jnp.zeros((tokens, TILE), F32)

        def add(start, source, column, width, square):
            rows = arrived[source, :, :, column:column + width].reshape(WIN * IMG, width)
            deep = lax.dot_general(
                hot, rows, (((0,), (0,)), ((), ())),
                preferred_element_type=F32,
            )
            total = (residual[0, :, start:start + width].astype(F32) + deep).astype(BF16)
            out[0, :, start:start + width] = total
            total = total.astype(F32)
            for i in range(0, width, TILE):
                piece = total[:, i:i + TILE]
                square = square + piece * piece
            return square

        for source in range(16):
            sx, sy = source // 4, source % 4
            base = ((sx // 2) * 4 + sy) * 640
            square = add(base + 384 * (sx % 2), source, 0 if lvl == 0 else 384, 256, square)
            if sx % 2 == lvl:
                square = add(base + 256, source, 256, 128, square)
        mean = jnp.sum(square, axis=1, keepdims=True) * (1.0 / 5120)
        scale = lax.rsqrt(mean + 1e-06)
        for start in range(0, 5120, 512):
            cols = slice(start, start + 512)
            values = out[0, :, cols].astype(F32)
            out[0, :, cols] = (values * scale * gain[lvl:lvl + 1, cols].astype(F32)).astype(BF16)

    @pl.when(level == 0)
    def _():
        for_level(0)

    @pl.when(level == 1)
    def _():
        for_level(1)


def per_device(
    vit_hidden, merge_weight, merge_bias, residual, norm_gain, image_sequence, token_source
):
    vit = vit_hidden.reshape(2 * ROWS, K)
    bias = jnp.pad(merge_bias.astype(F32), ((0, 6), (0, 0)))
    seq = jnp.broadcast_to(jnp.pad(image_sequence, (0, 4), constant_values=-1)[:, None], (32, 128))
    tokens = token_source.reshape(16, 128)
    any_, vmem = pl.BlockSpec(memory_space=pl.ANY), pl.BlockSpec(memory_space=pltpu.VMEM)
    arrived, keys = pl.pallas_call(
        exchange,
        name="exchange",
        out_shape=(
            jax.ShapeDtypeStruct((16, WIN, IMG, UNITS * TILE), BF16),
            jax.ShapeDtypeStruct((8, 128), I32),
        ),
        in_specs=[any_, any_, vmem, vmem, vmem],
        out_specs=(any_, vmem),
        scratch_shapes=[
            pltpu.VMEM((16, 2 * ROWS, K), BF16),
            pltpu.VMEM((8, 2, 2, 144, UNITS * TILE), BF16),
        ]
        + [pltpu.VMEM((64 * IMGS, IMG, TILE), BF16)] * UNITS
        + [
            pltpu.VMEM((UNITS, 16, WIN, IMG, TILE), BF16),
            pltpu.VMEM((256, 256), F32),
            pltpu.VMEM((HALF, 256), F32),
            pltpu.VMEM((8, 640), F32),
            pltpu.VMEM((32, 8, 128), I32),
            pltpu.VMEM((16, 8, 128), I32),
            pltpu.SMEM((16, 8, 128), I32),
            pltpu.SemaphoreType.DMA((SENDS + 40,)),
            pltpu.SemaphoreType.DMA((SENDS + 40,)),
            pltpu.SemaphoreType.DMA((2,)),
            pltpu.SemaphoreType.DMA((2, 3)),
            pltpu.SemaphoreType.DMA((2, 3)),
            pltpu.SemaphoreType.DMA((16,)),
            pltpu.SemaphoreType.DMA((16,)),
            pltpu.SemaphoreType.DMA((UNITS, 16)),
            pltpu.SemaphoreType.DMA((UNITS, 16)),
        ],
        compiler_params=pltpu.CompilerParams(
            collective_id=0, has_side_effects=True, vmem_limit_bytes=60 << 20
        ),
        cost_estimate=pl.CostEstimate(
            flops=2 * 2 * 448 * K * 640, bytes_accessed=8 << 20, transcendentals=0
        ),
    )(vit, merge_weight, bias, seq, tokens)
    count = residual.shape[1]
    return pl.pallas_call(
        finish,
        name="finish",
        grid=(2,),
        out_shape=jax.ShapeDtypeStruct(residual.shape, BF16),
        in_specs=[
            pl.BlockSpec((8, 128), lambda i: (0, 0)),
            pl.BlockSpec((16, WIN, IMG, UNITS * TILE), lambda i: (0, 0, 0, 0)),
            pl.BlockSpec((1, count, 5120), lambda i: (i, 0, 0)),
            pl.BlockSpec((2, 5120), lambda i: (0, 0)),
        ],
        out_specs=pl.BlockSpec((1, count, 5120), lambda i: (i, 0, 0)),
        compiler_params=pltpu.CompilerParams(vmem_limit_bytes=48 << 20),
    )(keys, arrived, residual, norm_gain)


def solution(mesh):
    return jax.shard_map(
        per_device,
        mesh=mesh,
        in_specs=(
            P(None, ("enc", "tp"), None),
            P(None, "enc", "tp"),
            P(None, "tp"),
            P(None, ("enc", "tp"), None),
            P(),
            P("enc"),
            P("enc"),
        ),
        out_specs=P(None, ("enc", "tp"), None),
        check_vma=False,
    )
```

time: 578 us -> 225 us (0.39)
  waiting for transfers between devices: 397 us -> 0 us
  Pallas kernels: 0 us -> 219 us
  blocking collectives: 72.8 us -> 0 us
  local copies, waits for them, and re-layouts: 40.9 us -> 4.51 us
  other arithmetic: 19.9 us -> 1.29 us
  starting transfers between devices: 16.1 us -> 0 us
  matrix products: 14.6 us -> 0 us
  between operations: 13.3 us -> 0.03 us
    all_gather x4 -> x0, waiting for transfers between devices: 331 us -> none  [the longest x2 204 us: per_device(): gathered = lax.all_gather(vit_hidden[level], 'tp', axis=0, tiled=True)]
    pallas_call x0 -> x2, Pallas kernels: none -> 219 us  [the longest x1 210 us: per_device(): pl.pallas_call(exchange, name='exchange', out_shape=(jax.ShapeDtypeStruct...]
    all_to_all x1 -> x0, blocking collectives: 72.8 us -> none  [per_device(): lax.all_to_all(sequence_rows, 'tp', split_axis=0, concat_axis=1, tiled=True)]
    all_to_all x3 -> x0, waiting for transfers between devices: 65 us -> none  [the longest x1 43.8 us: per_device(): lax.all_to_all(sequence_rows, 'tp', split_axis=0, concat_axis=1, tiled=True)]
    gather x2 -> x0, local copies, waits for them, and re-layouts: 18.7 us -> none  [place_tokens(): return jnp.take(padded, index, axis=0)]
    all_to_all x3 -> x0, starting transfers between devices: 16 us -> none  [the longest x2 12.1 us: per_device(): lax.all_to_all(outgoing, 'enc', split_axis=0, concat_axis=0, tiled=True)]
    dot_general x2 -> x0, matrix products: 14.6 us -> none  [accumulate(): return jnp.dot(gathered, piece, preferred_element_type=jnp.float32)]
    scatter x2 -> x0, local copies, waits for them, and re-layouts: 9.41 us -> none  [pack_slots(): slots = slots.at[destinations, ranks].set(grouped)]
  transfers between devices with their start and end apart: 7 -> 0, of which waited for: 6 -> 0; matrix products, arithmetic and copies ran while one was open for 7% -> 0% of each run, Pallas kernels for 0% -> 0%
where the time goes in v1:
time: 225 us
  Pallas kernels  219 us (97%)
  local copies, waits for them, and re-layouts  4.51 us (2%)
    pallas_call x1, Pallas kernels, per_device(): pl.pallas_call(exchange, name='exchange', out_shape=(jax.ShapeDtypeStruct...  210 us
    pallas_call x1, Pallas kernels, per_device(): pl.pallas_call(finish, name='finish', grid=(2,), out_shape=jax.ShapeDtype...  9.08 us

profile of v1, /device:TPU:32, one launch (start us, length us, event | category | flops | bytes accessed | tf_op | source)
XLA Modules:
  0.0 224.6 jit_solution(12251339505333721252)
XLA Ops:
  0.0 0.7 pad.12
  0.7 0.7 broadcast_in_dim.2.seq
  1.3 1.3 pad_convert_fusion.bias
  2.6 0.0 copy-start.1
  2.6 209.7 %exchange.1 = (bf16[16,17,16,640]{3,2,1,0:T(8,128)(2,1)}, s32[8,128]{1,0:T(8,128)}) custom-call(bf16[112,4608]{1,0:T(8,128)(2,1)} %bitcast.2, bf16[2,144,640]{2,1,0:T(8,128)(2,1)} %w.1, f32[8,640]{1,0:T(8,128)} %pad_convert_fusion.bias, s32[32,128]{1,0:T(8,128)} %broadcast_in_dim.2.seq, s32[16,128]{1,0:T(8,128)} %bitcast.3), custom_call_target="tpu_custom_call" | custom-call | flops 5284823040 | bytes 8388608 | tf_op jit(solution)/shard_map/exchange/pallas_call | solution.py:573
  212.4 0.0 copy-done.1
  212.4 0.0 copy-start
  212.4 2.5 %copy-done = bf16[2,256,5120]{2,1,0:T(8,128)(2,1)S(1)} copy-done((bf16[2,256,5120]{2,1,0:T(8,128)(2,1)S(1)}, bf16[2,256,5120]{2,1,0:T(8,128)(2,1)}, u32[]{:S(2)}) %copy-start) | copy-done | bytes 5242904
  214.9 0.0 copy-start.2
  214.9 0.7 copy-done.2
  215.6 9.1 %finish.1 = bf16[2,256,5120]{2,1,0:T(8,128)(2,1)} custom-call(s32[8,128]{1,0:T(8,128)S(1)} %copy-done.2, bf16[16,17,16,640]{3,2,1,0:T(8,128)(2,1)} %get-tuple-element.8.arrived, bf16[2,256,5120]{2,1,0:T(8,128)(2,1)S(1)} %copy-done, bf16[2,5120]{1,0:T(2,128)(2,1)S(1)} %copy-done.1), custom_call_target="tpu_custom_call" | custom-call | tf_op jit(solution)/shard_map/finish/pallas_call | solution.py:613
Async XLA Ops:
  2.6 209.7 %copy-start.1 = (bf16[2,5120]{1,0:T(2,128)(2,1)S(1)}, bf16[2,5120]{1,0:T(2,128)(2,1)}, u32[]{:S(2)}) copy-start(bf16[2,5120]{1,0:T(2,128)(2,1)} %gain.1) | copy-start | bytes 61444
  212.4 2.5 %copy-start = (bf16[2,256,5120]{2,1,0:T(8,128)(2,1)S(1)}, bf16[2,256,5120]{2,1,0:T(8,128)(2,1)}, u32[]{:S(2)}) copy-start(bf16[2,256,5120]{2,1,0:T(8,128)(2,1)} %residual.1) | copy-start | bytes 15728644
  214.9 0.7 copy-start.2

commit v2 on v1

--- a/solution.py
+++ b/solution.py
@@ -18,7 +18,7 @@
 K = 4608
 TILE = 128
 UNITS = 5
-SENDS = 160
+SENDS = 300
 
 
 def place(enc, tp):
@@ -42,9 +42,9 @@
 
 
 def exchange(
-    vit, w, bias, seq, tokens,
+    vit, w, bias, images, tokens,
     arrived, keys,
-    held, weight, g0, g1, g2, g3, g4, staged, acc, joined, other_bias, table, lists, list_s,
+    held, weight, g0, g1, g2, g3, g4, staged, acc, joined, own_bias, other_bias, table, lists, list_s,
     ssem, rsem, lsem, ws, wr, ls, lr, ds, dr,
 ):
     gathered = (g0, g1, g2, g3, g4)
@@ -67,37 +67,38 @@
     def at_lo(d):
         return device(lax.rem(z_lo + d, 4), x, core, z_hi, y)
 
-    def scatter_to(b):
-        return device(z_lo, 2 * z_hi + b, core, x_half, y)
+    def scatter_to(b, i):
+        side = 1 - z_hi if i == 2 else z_hi
+        return device(z_lo, 2 * side + b, core, x_half, y)
 
     far = x_half != z_hi
 
     barrier = pltpu.get_barrier_semaphore()
     peers = [at_xy(d // 4, d % 4) for d in range(1, 16)]
     peers += [at_z(1), at_z(-1), sibling, across] + [at_lo(d) for d in (1, 2, 3)]
-    for peer in peers:
+    senders = [device(z_lo, 2 * z_hi + i, core, 1 - z_hi, y) for i in range(2)]
+    for peer in peers + senders:
         pl.semaphore_signal(barrier, inc=1, device_id=peer, device_id_type=MESH)
-
-    @pl.when(far)
-    def _():
-        for b in range(2):
-            pl.semaphore_signal(barrier, inc=1, device_id=scatter_to(b), device_id_type=MESH)
-
-    pl.semaphore_wait(barrier, len(peers) + jnp.where(far, 2, 0))
-
-    sends = []
-
-    def put(src, dst, to):
-        number = len(sends)
-        copy = pltpu.make_async_remote_copy(
-            src_ref=src, dst_ref=dst, send_sem=ssem.at[number], recv_sem=rsem.at[number],
-            device_id=to, device_id_type=MESH,
+    pl.semaphore_wait(barrier, len(peers) + jnp.where(far, 4, 0))
+
+    sends = {}
+
+    def descriptor(key):
+        number, like = sends[key]
+        return pltpu.make_async_remote_copy(
+            src_ref=like(), dst_ref=like(), send_sem=ssem.at[number], recv_sem=rsem.at[number],
+            device_id=sibling, device_id_type=MESH,
         )
-        copy.start()
-        sends.append(copy)
-        return number
-
-    def got(number, dst):
+
+    def put(key, src, like, to, dst=None):
+        number = sends.setdefault(key, (len(sends), like))[0]
+        pltpu.make_async_remote_copy(
+            src_ref=src, dst_ref=like() if dst is None else dst, send_sem=ssem.at[number],
+            recv_sem=rsem.at[number], device_id=to, device_id_type=MESH,
+        ).start()
+
+    def got(key, dst):
+        number = sends[key][0]
         pltpu.make_async_remote_copy(
             src_ref=dst, dst_ref=dst, send_sem=ssem.at[number], recv_sem=rsem.at[number],
             device_id=sibling, device_id_type=MESH,
@@ -116,8 +117,6 @@
 
     def step_to(p, axis, d):
         return at_xy(*(near(p, d, 0) if axis == 0 else near(p, 0, d)))
-
-    ids = {}
 
     def send_block(level, p, axis, d, first, second, half=None, src=None):
         if axis == 0:
@@ -125,17 +124,15 @@
         else:
             there = (first, (second - d) % 4)
         src = block(level, p, *near(p, first, second), half) if src is None else src
-        ids[(level, p, there, half)] = put(
-            src, block(level, p, *near(p, *there), half), step_to(p, axis, d)
-        )
+        put(("v", level, p, there, half), src, lambda: block(level, p, *near(p, *there), half), step_to(p, axis, d))
 
     def have(level, p, first, second, half=None):
-        got(ids[(level, p, (first, second), half)], block(level, p, *near(p, first, second), half))
-
-    def vit_own(level):
+        got(("v", level, p, (first, second), half), block(level, p, *near(p, first, second), half))
+
+    def vit_own(level, ways=((0, 0), (0, 1), (1, 0), (1, 1))):
         rows = pl.ds(0, 64) if level == 0 else pl.ds(64, 48)
-        for axis in range(2):
-            for p in range(2):
+        for axis, p in ways:
+            if True:
                 for d in (1, -1):
                     send_block(level, p, axis, d, 0, 0, src=vit.at[rows, pl.ds(p * part, part)])
 
@@ -161,21 +158,21 @@
                     have(level, p, 2, 0, half)
                 for d2 in (1, -1):
                     send_block(level, p, 1, d2, 2, 0)
-        if number == 4:
-            for first in (3, 1):
+        if number in (4, 5):
+            for first in ((3,) if number == 4 else (1,)):
                 for p in both:
                     for d in (1, -1):
                         off = (-d) % 4
                         have(level, p, first, off)
                         send_block(level, p, 1, d, first, off, half=0 if d == 1 else 1)
-        if number == 5:
+        if number == 6:
             for p in both:
                 for d in (1, -1):
                     off = (-d) % 4
                     have(level, p, 2, off)
                     send_block(level, p, 1, d, 2, off, half=0 if d == 1 else 1)
-        if number == 6:
-            for first in (0, 3, 1, 2):
+        if number in (7, 8):
+            for first in ((0,) if number == 7 else (3, 1, 2)):
                 for p in both:
                     for half in both:
                         have(level, p, first, 2, half)
@@ -192,7 +189,7 @@
         src, dst = scatter_parts(b)[i]
         return pltpu.make_async_remote_copy(
             src_ref=src, dst_ref=dst, send_sem=ws.at[b, i], recv_sem=wr.at[odd, i],
-            device_id=scatter_to(b), device_id_type=MESH,
+            device_id=scatter_to(b, i), device_id_type=MESH,
         )
 
     def stays(b):
@@ -202,90 +199,93 @@
         for b in range(2):
             @pl.when(stays(b))
             def _():
-                for i, (src, dst) in enumerate(scatter_parts(b)):
+                for i, (src, dst) in enumerate(scatter_parts(b)[:2]):
                     pltpu.make_async_copy(src, dst, wr.at[odd, i]).start()
 
             @pl.when(jnp.logical_not(stays(b)))
             def _():
-                for i in range(3):
+                for i in range(2):
                     scatter_copy(b, i).start()
-
-    def rows_of(d, whose=None):
-        there = lax.rem(z + d + 8, 8)
-        index = lax.rem(there, 4) * 2 + lax.div(there, 4)
-        return weight.at[index, :, core if whose is None else whose]
-
-    wid = {}
-
-    def ring_send(kind, store, view, d, up):
+        for b in range(2):
+            scatter_copy(b, 2).start()
+
+    wide = ((0, 384), (384, 256))
+
+    def ring_send(kind, view, d, up):
         to = at_z(1) if up else at_z(-1)
         there = d - 1 if up else d + 1
-        if abs(there) == 4:
-            piece = view(d, 0 if up else 1)
-        else:
-            piece = view(d, None)
-        store[(kind, there)] = put(piece, piece, to)
-
-    def weight_view(d, half):
-        there = lax.rem(z + d + 8, 8)
-        index = lax.rem(there, 4) * 2 + lax.div(there, 4)
-        if half is None:
-            return weight.at[index, :, core]
-        return weight.at[index, half, core]
-
-    def weight_step(number):
+        half = None if abs(there) < 4 else 0 if up else 1
+        put((kind, there), view(d, half), lambda: view(d, half), to)
+
+    def core_send(kind, view, d):
+        put((kind, "core", d), view(d, None), lambda: view(d, None), sibling)
+
+    def weight_view(part_, whose):
+        cols = pl.ds(*wide[part_])
+
+        def view(d, half):
+            there = lax.rem(z + d + 8, 8)
+            index = lax.rem(there, 4) * 2 + lax.div(there, 4)
+            if half is None:
+                return weight.at[index, :, whose, :, cols]
+            return weight.at[index, half, whose, :, cols]
+        return view
+
+    def weight_step(part_, number):
+        view = weight_view(part_, core)
+        kind = ("w", part_)
         if number == 0:
             for i in range(2):
-                for k, cols in enumerate(((0, 256), (256, 128), (384, 256))):
+                for k, cols in (((0, (0, 256)), (1, (256, 128))), ((2, (384, 256)),))[part_]:
                     landing = weight.at[z_lo * 2 + z_hi, i, core, :, pl.ds(*cols)]
                     pltpu.make_async_remote_copy(
                         src_ref=landing, dst_ref=landing, send_sem=ws.at[0, k], recv_sem=wr.at[i, k],
                         device_id=sibling, device_id_type=MESH,
                     ).wait_recv()
             for up in (True, False):
-                ring_send("w", wid, weight_view, 0, up)
-            wid[("s", 0)] = put(weight_view(0, None), weight_view(0, None), sibling)
+                ring_send(kind, view, 0, up)
+            core_send(kind, view, 0)
+        elif number < 5:
+            ring_step(kind, view, number)
         else:
-            ring_step("w", wid, weight_view, number)
-            if number == 4:
-                for d in (0, -1, 1, -2, 2, -3, 3, 4):
-                    got(wid[("s", d)], rows_of(d, 1 - core))
-
-    def ring_step(kind, store, view, number):
+            for d in (0, -1, 1, -2, 2, -3, 3, 4):
+                got((kind, "core", d), weight_view(part_, 1 - core)(d, None))
+
+    def ring_step(kind, view, number):
         if number < 4:
             for d, up in ((-number, True), (number, False)):
-                got(store[(kind, d)], view(d, None))
-                ring_send(kind, store, view, d, up)
-                store[("s", d)] = put(view(d, None), view(d, None), sibling)
+                got((kind, d), view(d, None))
+                ring_send(kind, view, d, up)
+                core_send(kind, view, d)
         else:
-            got(store[(kind, -4)], view(-4, 0))
-            got(store[(kind, 4)], view(4, 1))
-            store[("s", 4)] = put(view(4, None), view(4, None), sibling)
-
-    def merged_view(g, d, half, whose):
-        start = (whose * 8 + lax.rem(z + d + 8, 8)) * (4 * IMGS)
+            got((kind, -4), view(-4, 0))
+            got((kind, 4), view(4, 1))
+            core_send(kind, view, 4)
+
+    def merged_view(g, group, d, half, whose):
+        count = IMGS if group == 0 else 3 * IMGS
+        start = (whose * 8 + lax.rem(z + d + 8, 8)) * (4 * IMGS) + group * IMGS
         if half is None:
-            return g.at[pl.ds(start, 4 * IMGS)]
-        return g.at[pl.ds(start + half * 2 * IMGS, 2 * IMGS)]
-
-    gid = [dict() for _ in range(UNITS)]
-
-    def unit_view(unit):
-        return lambda d, half: merged_view(gathered[unit], d, half, core)
-
-    def unit_step(unit, number):
-        view = unit_view(unit)
+            return g.at[pl.ds(start, count)]
+        return g.at[pl.ds(start + half * (count // 2), count // 2)]
+
+    def unit_step(unit, group, number):
+        kind = ("g", unit, group)
+
+        def view(d, half):
+            return merged_view(gathered[unit], group, d, half, core)
+
         if number == 0:
             for up in (True, False):
-                ring_send("g", gid[unit], view, 0, up)
-            gid[unit][("s", 0)] = put(view(0, None), view(0, None), sibling)
+                ring_send(kind, view, 0, up)
+            core_send(kind, view, 0)
         elif number < 5:
-            ring_step("g", gid[unit], view, number)
+            ring_step(kind, view, number)
         else:
             for d in (0, -1, 1, -2, 2, -3, 3, 4):
-                got(gid[unit][("s", d)], merged_view(gathered[unit], d, None, 1 - core))
-
-    def project(level, column, width, units, bias_row):
+                got((kind, "core", d), merged_view(gathered[unit], group, d, None, 1 - core))
+
+    def project(group, level, column, width, units, bias_row):
         def one(r, _):
             def chunk(k, _):
                 rows = held[pl.ds(r * 4, 4), pl.ds(pl.multiple_of(level * 48, 16), 64),
@@ -310,7 +310,7 @@
                 joined[pl.ds(start, ROWS), :width] = acc[
                     pl.ds(pl.multiple_of(ry * 64 + level * 8, 8), ROWS), :width
                 ]
-            start = ((core * 8 + z) * 4 + lax.rem(x + r, 4)) * IMGS
+            start = ((core * 8 + z) * 4 + r) * IMGS
             for i, unit in enumerate(units):
                 cols = slice(i * TILE, (i + 1) * TILE)
                 gathered[unit][pl.ds(start, IMGS)] = (
@@ -318,10 +318,10 @@
                 ).astype(BF16).reshape(IMGS, IMG, TILE)
             return 0
 
-        lax.fori_loop(0, 4, one, 0)
+        lax.fori_loop(*((0, 1) if group == 0 else (1, 4)), one, 0)
 
     def bias_of(level, column, width):
-        mine = jnp.where(far, other_bias[...], bias[...])
+        mine = jnp.where(jnp.logical_xor(far, column is None and level == 1), other_bias[...], own_bias[...])
         row = jnp.where(level == 0, mine[0:1], mine[1:2])
         if column is None:
             return jnp.where(odd == 0, row[:, 0:width], row[:, 384:384 + width])
@@ -373,9 +373,12 @@
     sub = lax.broadcasted_iota(I32, (32, 128), 0)
 
     def own_table():
-        ours = jnp.where(seq[...] == lax.div(lane, 2), 1, 0)
+        of = jnp.full((32, 128), -1, I32)
+        for i in range(2 * IMGS):
+            of = jnp.where(sub == i, images[i], of)
+        ours = jnp.where(of == lax.div(lane, 2), 1, 0)
         second = jnp.where(sub >= 14, 1, 0)
-        where = ((core * 8 + second * 4 + z_lo) * 4 + x) * 14 + sub - 14 * second
+        where = ((core * 8 + second * 4 + z_lo) * 16 + sub - IMGS * second) * 4 + x
         pick = jnp.logical_and(ours == 1, running(ours) == lax.rem(lane, 2))
         row = jnp.sum(jnp.where(pick, where, 0), axis=0, keepdims=True)
         table[enc] = jnp.broadcast_to(row, (8, 128))
@@ -424,103 +427,192 @@
             copy.wait_recv()
             return 0
         lax.fori_loop(1, 16, one, 0)
+        value = lists[...]
+        r = jnp.bitwise_and(jnp.bitwise_and(value, 3) + (4 - x), 3)
+        image = jnp.bitwise_and(lax.shift_right_logical(value, 2), 15)
+        lists[...] = (lax.shift_right_logical(value, 6) * 4 + r) * IMGS + image
         copy = pltpu.make_async_copy(lists, list_s, lsem.at[1])
         copy.start()
         copy.wait()
 
+    weight_scatter()
     vit_own(0)
     mine = pltpu.make_async_copy(vit, held.at[0], lsem.at[0])
     mine.start()
-    weight_scatter()
-    bias_id = put(bias, other_bias, across)
     own_table()
+    own_bias[...] = jnp.zeros((8, 640), F32)
+    own_bias[0:2, :] = bias[...].astype(F32)
     own = table.at[enc]
-    sib_id = put(own, own, sibling)
+    put("one", own, lambda: own, sibling)
+    put("bias", own_bias, lambda: other_bias, across)
     vit_step(0, 1)
-    weight_step(0)
-    got(sib_id, table.at[z_lo * 8 + x * 2 + 1 - core])
+    weight_step(0, 0)
+    weight_step(1, 0)
+    vit_step(0, 2)
+    got("one", table.at[z_lo * 8 + x * 2 + 1 - core])
     pair = table.at[pl.ds(z_lo * 8 + x * 2, 2)]
-    pair_ids = [put(pair, pair, at_xy(d, 0)) for d in (1, 2, 3)]
-    vit_step(0, 2)
-    for d, number in zip((1, 2, 3), pair_ids):
-        got(number, table.at[pl.ds(z_lo * 8 + lax.rem(x - d + 4, 4) * 2, 2)])
+    for d in (1, 2, 3):
+        put(("pair", d), pair, lambda: pair, at_xy(d, 0))
+    weight_step(0, 1)
+    weight_step(1, 1)
+    weight_step(0, 2)
+    vit_step(0, 3)
+    vit_step(0, 4)
+    vit_step(0, 5)
+    weight_step(1, 2)
+    weight_step(0, 3)
+    vit_step(0, 7)
+    weight_step(1, 3)
+    for d in (1, 2, 3):
+        got(("pair", d), table.at[pl.ds(z_lo * 8 + lax.rem(x - d + 4, 4) * 2, 2)])
     eight = table.at[pl.ds(z_lo * 8, 8)]
-    lo_ids = [put(eight, eight, at_lo(d)) for d in (1, 2, 3)]
-    weight_step(1)
-    vit_step(0, 3)
-    for d, number in zip((1, 2, 3), lo_ids):
-        got(number, table.at[pl.ds(lax.rem(z_lo - d + 4, 4) * 8, 8)])
+    for d in (1, 2, 3):
+        put(("eight", d), eight, lambda: eight, at_lo(d))
+    weight_step(0, 4)
+    vit_step(0, 6)
+    vit_own(1)
+    weight_step(1, 4)
+    weight_step(0, 5)
+    weight_step(1, 5)
+    mine.wait()
+    got("bias", other_bias)
+    a = (0, 0, 256, (0, 1), bias_of(0, None, 256))
+    project(0, *a)
+    unit_step(0, 0, 0)
+    unit_step(1, 0, 0)
+    unit_step(0, 0, 1)
+    unit_step(1, 0, 1)
+    vit_step(0, 8)
+    project(1, *a)
+    unit_step(0, 1, 0)
+    unit_step(1, 1, 0)
+    unit_step(0, 0, 2)
+    unit_step(1, 0, 2)
+    for d in (1, 2, 3):
+        got(("eight", d), table.at[pl.ds(lax.rem(z_lo - d + 4, 4) * 8, 8)])
     own_list()
     list_send()
-    weight_step(2)
-    vit_step(0, 4)
-    vit_own(1)
-    weight_step(3)
-    vit_step(0, 5)
-    list_wait()
-    got(bias_id, other_bias)
-    weight_step(4)
-    mine.wait()
-    vit_step(0, 6)
-    project(0, 0, 256, (0, 1), bias_of(0, None, 256))
-    unit_step(0, 0)
-    unit_step(1, 0)
-    vit_step(1, 1)
-    unit_step(0, 1)
-    vit_step(1, 2)
-    unit_step(1, 1)
-    vit_step(1, 3)
-    unit_step(0, 2)
-    vit_step(1, 4)
-    unit_step(1, 2)
-    vit_step(1, 5)
-    unit_step(0, 3)
-    unit_step(1, 3)
-    vit_step(1, 6)
-    project(odd, 256, 128, (2,), bias_of(odd, 256, 128))
-    unit_step(2, 0)
-    project(1, 384, 256, (3, 4), bias_of(1, None, 256))
-    unit_step(3, 0)
-    unit_step(0, 4)
-    unit_step(1, 4)
-    unit_step(0, 5)
-    unit_step(2, 1)
-    window_send(0)
-    unit_step(3, 1)
-    unit_step(2, 2)
-    unit_step(1, 5)
-    window_send(1)
-    unit_step(3, 2)
-    unit_step(4, 0)
-    unit_step(2, 3)
-    unit_step(3, 3)
-    unit_step(4, 1)
-    unit_step(2, 4)
-    unit_step(3, 4)
-    unit_step(4, 2)
-    unit_step(2, 5)
-    window_send(2)
-    unit_step(3, 5)
-    window_send(3)
-    unit_step(4, 3)
-    unit_step(4, 4)
-    unit_step(4, 5)
-    window_send(4)
+
+    def window(unit):
+        unit_step(unit, 0, 5)
+        unit_step(unit, 1, 5)
+        window_send(unit)
+
+    def rest(even):
+        b = (0 if even else 1, 256, 128, (2,), bias_of(0 if even else 1, 256, 128))
+        c = (1, 384, 256, (3, 4), bias_of(1, None, 256))
+        few = (3, 4) if even else (2, 3, 4)
+
+        def small(number):
+            for unit in few:
+                unit_step(unit, 0, number)
+
+        vit_step(1, 1)
+        vit_step(1, 2)
+        if even:
+            project(0, *b)
+            project(1, *b)
+        unit_step(0, 0, 3)
+        unit_step(1, 0, 3)
+        unit_step(0, 1, 1)
+        unit_step(1, 1, 1)
+        unit_step(0, 0, 4)
+        unit_step(1, 0, 4)
+        if even:
+            unit_step(2, 0, 0)
+            unit_step(2, 1, 0)
+        unit_step(0, 1, 2)
+        vit_step(1, 3)
+        unit_step(1, 1, 2)
+        vit_step(1, 7)
+        vit_step(1, 4)
+        vit_step(1, 5)
+        if not even:
+            project(0, *b)
+            unit_step(2, 0, 0)
+        project(0, *c)
+        unit_step(3, 0, 0)
+        unit_step(4, 0, 0)
+        unit_step(0, 1, 3)
+        vit_step(1, 6)
+        unit_step(1, 1, 3)
+        unit_step(0, 1, 4)
+        list_wait()
+        window(0)
+        vit_step(1, 8)
+        if even:
+            project(1, *c)
+            unit_step(3, 1, 0)
+            unit_step(1, 1, 4)
+            window(1)
+            unit_step(2, 0, 1)
+            unit_step(2, 1, 1)
+            small(1)
+            unit_step(2, 0, 2)
+            unit_step(2, 1, 2)
+            unit_step(3, 1, 1)
+            small(2)
+            unit_step(2, 0, 3)
+            unit_step(2, 1, 3)
+            unit_step(3, 1, 2)
+            unit_step(4, 1, 0)
+            small(3)
+            unit_step(2, 0, 4)
+            unit_step(2, 1, 4)
+            window(2)
+            small(4)
+        else:
+            project(1, *b)
+            unit_step(2, 1, 0)
+            unit_step(1, 1, 4)
+            window(1)
+            small(1)
+            project(1, *c)
+            unit_step(2, 1, 1)
+            small(2)
+            unit_step(2, 1, 2)
+            unit_step(3, 1, 0)
+            small(3)
+            unit_step(2, 1, 3)
+            small(4)
+            unit_step(3, 1, 1)
+            unit_step(2, 1, 4)
+            unit_step(4, 1, 0)
+            window(2)
+            unit_step(3, 1, 2)
+        unit_step(3, 1, 3)
+        unit_step(4, 1, 1)
+        unit_step(3, 1, 4)
+        window(3)
+        unit_step(4, 1, 2)
+        unit_step(4, 1, 3)
+        unit_step(4, 1, 4)
+        window(4)
+
+    @pl.when(odd == 0)
+    def _():
+        rest(True)
+
+    @pl.when(odd == 1)
+    def _():
+        rest(False)
+
     for unit in range(UNITS):
         window_wait(unit)
-    for copy in sends:
-        copy.wait_send()
+    for key in sends:
+        descriptor(key).wait_send()
     for b in range(2):
         @pl.when(jnp.logical_not(stays(b)))
         def _():
-            for i in range(3):
+            for i in range(2):
                 scatter_copy(b, i).wait_send()
+        scatter_copy(b, 2).wait_send()
 
 
 def finish(keys, arrived, residual, gain, out):
     level = pl.program_id(0)
     tokens = residual.shape[1]
-    key = jnp.concatenate([keys[0:1, :], keys[1:2, :]], axis=1)
+    key = keys[pl.ds(pl.program_id(1), 1), :]
     hot = jnp.where(lax.broadcasted_iota(I32, (WIN * IMG, tokens), 0) == key, 1.0, 0.0).astype(BF16)
 
     def for_level(lvl):
@@ -543,7 +635,11 @@
         for source in range(16):
             sx, sy = source // 4, source % 4
             base = ((sx // 2) * 4 + sy) * 640
-            square = add(base + 384 * (sx % 2), source, 0 if lvl == 0 else 384, 256, square)
+            other = ((1 - sx // 2) * 4 + sy) * 640
+            if lvl == 0:
+                square = add(base + 384 * (sx % 2), source, 0, 256, square)
+            else:
+                square = add(other + 384 * (sx % 2), source, 384, 256, square)
             if sx % 2 == lvl:
                 square = add(base + 256, source, 256, 128, square)
         mean = jnp.sum(square, axis=1, keepdims=True) * (1.0 / 5120)
@@ -566,8 +662,6 @@
     vit_hidden, merge_weight, merge_bias, residual, norm_gain, image_sequence, token_source
 ):
     vit = vit_hidden.reshape(2 * ROWS, K)
-    bias = jnp.pad(merge_bias.astype(F32), ((0, 6), (0, 0)))
-    seq = jnp.broadcast_to(jnp.pad(image_sequence, (0, 4), constant_values=-1)[:, None], (32, 128))
     tokens = token_source.reshape(16, 128)
     any_, vmem = pl.BlockSpec(memory_space=pl.ANY), pl.BlockSpec(memory_space=pltpu.VMEM)
     arrived, keys = pl.pallas_call(
@@ -577,7 +671,7 @@
             jax.ShapeDtypeStruct((16, WIN, IMG, UNITS * TILE), BF16),
             jax.ShapeDtypeStruct((8, 128), I32),
         ),
-        in_specs=[any_, any_, vmem, vmem, vmem],
+        in_specs=[any_, any_, vmem, pl.BlockSpec(memory_space=pltpu.SMEM), vmem],
         out_specs=(any_, vmem),
         scratch_shapes=[
             pltpu.VMEM((16, 2 * ROWS, K), BF16),
@@ -589,11 +683,12 @@
             pltpu.VMEM((256, 256), F32),
             pltpu.VMEM((HALF, 256), F32),
             pltpu.VMEM((8, 640), F32),
+            pltpu.VMEM((8, 640), F32),
             pltpu.VMEM((32, 8, 128), I32),
             pltpu.VMEM((16, 8, 128), I32),
             pltpu.SMEM((16, 8, 128), I32),
-            pltpu.SemaphoreType.DMA((SENDS + 40,)),
-            pltpu.SemaphoreType.DMA((SENDS + 40,)),
+            pltpu.SemaphoreType.DMA((SENDS,)),
+            pltpu.SemaphoreType.DMA((SENDS,)),
             pltpu.SemaphoreType.DMA((2,)),
             pltpu.SemaphoreType.DMA((2, 3)),
             pltpu.SemaphoreType.DMA((2, 3)),
@@ -608,21 +703,21 @@
         cost_estimate=pl.CostEstimate(
             flops=2 * 2 * 448 * K * 640, bytes_accessed=8 << 20, transcendentals=0
         ),
-    )(vit, merge_weight, bias, seq, tokens)
+    )(vit, merge_weight, merge_bias, image_sequence, tokens)
     count = residual.shape[1]
     return pl.pallas_call(
         finish,
         name="finish",
-        grid=(2,),
+        grid=(2, 2),
         out_shape=jax.ShapeDtypeStruct(residual.shape, BF16),
         in_specs=[
-            pl.BlockSpec((8, 128), lambda i: (0, 0)),
-            pl.BlockSpec((16, WIN, IMG, UNITS * TILE), lambda i: (0, 0, 0, 0)),
-            pl.BlockSpec((1, count, 5120), lambda i: (i, 0, 0)),
-            pl.BlockSpec((2, 5120), lambda i: (0, 0)),
+            pl.BlockSpec((8, 128), lambda i, j: (0, 0)),
+            pl.BlockSpec((16, WIN, IMG, UNITS * TILE), lambda i, j: (0, 0, 0, 0)),
+            pl.BlockSpec((1, count // 2, 5120), lambda i, j: (i, j, 0)),
+            pl.BlockSpec((2, 5120), lambda i, j: (0, 0)),
         ],
-        out_specs=pl.BlockSpec((1, count, 5120), lambda i: (i, 0, 0)),
-        compiler_params=pltpu.CompilerParams(vmem_limit_bytes=48 << 20),
+        out_specs=pl.BlockSpec((1, count // 2, 5120), lambda i, j: (i, j, 0)),
+        compiler_params=pltpu.CompilerParams(vmem_limit_bytes=60 << 20),
     )(keys, arrived, residual, norm_gain)
 
 

time: 225 us -> 206 us (0.916)
  Pallas kernels: 219 us -> 204 us
  local copies, waits for them, and re-layouts: 4.51 us -> 0 us
    pallas_call x1, Pallas kernels: 210 us -> 193 us  [per_device(): pl.pallas_call(exchange, name='exchange', out_shape=(jax.ShapeDtypeStruct...]
    unnamed x6 -> x0, local copies, waits for them, and re-layouts: 3.17 us -> none
where the time goes in v2:
time: 206 us; the launch traced here: 204 us
  Pallas kernels  204 us (99%)
    pallas_call x1, Pallas kernels, per_device(): pl.pallas_call(exchange, name='exchange', out_shape=(jax.ShapeDtypeStruct...  193 us
    pallas_call x1, Pallas kernels, per_device(): pl.pallas_call(finish, name='finish', grid=(2, 2), out_shape=jax.ShapeDty...  10.2 us

profile of v2, /device:TPU:32, one launch (start us, length us, event | category | flops | bytes accessed | tf_op | source)
XLA Modules:
  0.0 203.6 jit_solution(5183656579955265124)
XLA Ops:
  0.0 193.4 %exchange.1 = (bf16[16,17,16,640]{3,2,1,0:T(8,128)(2,1)}, s32[8,128]{1,0:T(8,128)}) custom-call(bf16[112,4608]{1,0:T(8,128)(2,1)} %bitcast.2, bf16[2,144,640]{2,1,0:T(8,128)(2,1)} %w.1, bf16[2,640]{1,0:T(2,128)(2,1)} %bias.1, s32[28]{0:T(128)} %images.1, s32[16,128]{1,0:T(8,128)} %bitcast.3), custom_call_target="tpu_custom_call" | custom-call | flops 5284823040 | bytes 8388608 | tf_op jit(solution)/shard_map/exchange/pallas_call | solution.py:667
  193.4 10.2 %finish.1 = bf16[2,256,5120]{2,1,0:T(8,128)(2,1)} custom-call(s32[8,128]{1,0:T(8,128)} %get-tuple-element.7.keys, bf16[16,17,16,640]{3,2,1,0:T(8,128)(2,1)} %get-tuple-element.8.arrived, bf16[2,256,5120]{2,1,0:T(8,128)(2,1)} %residual.1, bf16[2,5120]{1,0:T(2,128)(2,1)} %gain.1), custom_call_target="tpu_custom_call" | custom-call | tf_op jit(solution)/shard_map/finish/pallas_call | solution.py:708

commit v3 on v2

--- a/solution.py
+++ b/solution.py
@@ -69,29 +69,28 @@
 
     def scatter_to(b, i):
         side = 1 - z_hi if i == 2 else z_hi
-        return device(z_lo, 2 * side + b, core, x_half, y)
+        return device(z_lo, 2 * side + b, core, z_hi, y)
 
     far = x_half != z_hi
 
     barrier = pltpu.get_barrier_semaphore()
     peers = [at_xy(d // 4, d % 4) for d in range(1, 16)]
     peers += [at_z(1), at_z(-1), sibling, across] + [at_lo(d) for d in (1, 2, 3)]
-    senders = [device(z_lo, 2 * z_hi + i, core, 1 - z_hi, y) for i in range(2)]
-    for peer in peers + senders:
+    for peer in peers:
         pl.semaphore_signal(barrier, inc=1, device_id=peer, device_id_type=MESH)
-    pl.semaphore_wait(barrier, len(peers) + jnp.where(far, 4, 0))
+    pl.semaphore_wait(barrier, len(peers))
 
     sends = {}
 
     def descriptor(key):
-        number, like = sends[key]
+        number, like, _ = sends[key]
         return pltpu.make_async_remote_copy(
             src_ref=like(), dst_ref=like(), send_sem=ssem.at[number], recv_sem=rsem.at[number],
             device_id=sibling, device_id_type=MESH,
         )
 
-    def put(key, src, like, to, dst=None):
-        number = sends.setdefault(key, (len(sends), like))[0]
+    def put(key, src, like, to, dst=None, when=None):
+        number = sends.setdefault(key, (len(sends), like, when))[0]
         pltpu.make_async_remote_copy(
             src_ref=src, dst_ref=like() if dst is None else dst, send_sem=ssem.at[number],
             recv_sem=rsem.at[number], device_id=to, device_id_type=MESH,
@@ -177,79 +176,107 @@
                     for half in both:
                         have(level, p, first, 2, half)
 
+    mine_w = weight.at[z_lo * 2 + x_half, odd, core]
+
     def scatter_parts(b):
-        mine = weight.at[z_lo * 2 + x_half, odd, core]
         return (
-            (w.at[0, :, pl.ds(384 * b, 256)], mine.at[:, pl.ds(0, 256)]),
-            (w.at[b, :, pl.ds(256, 128)], mine.at[:, pl.ds(256, 128)]),
-            (w.at[1, :, pl.ds(384 * b, 256)], mine.at[:, pl.ds(384, 256)]),
+            (w.at[0, :, pl.ds(384 * b, 256)], mine_w.at[:, pl.ds(0, 256)]),
+            (w.at[b, :, pl.ds(256, 128)], mine_w.at[:, pl.ds(256, 128)]),
+            (w.at[1, :, pl.ds(384 * b, 256)], mine_w.at[:, pl.ds(384, 256)]),
         )
 
     def scatter_copy(b, i):
         src, dst = scatter_parts(b)[i]
         return pltpu.make_async_remote_copy(
-            src_ref=src, dst_ref=dst, send_sem=ws.at[b, i], recv_sem=wr.at[odd, i],
+            src_ref=src, dst_ref=dst, send_sem=ws.at[b, i], recv_sem=wr.at[x, i],
             device_id=scatter_to(b, i), device_id_type=MESH,
         )
 
-    def stays(b):
-        return jnp.logical_and(2 * z_hi + b == x, jnp.logical_not(far))
+    def stays(b, i):
+        return jnp.logical_and(odd == b, far if i == 2 else jnp.logical_not(far))
 
     def weight_scatter():
         for b in range(2):
-            @pl.when(stays(b))
-            def _():
-                for i, (src, dst) in enumerate(scatter_parts(b)[:2]):
-                    pltpu.make_async_copy(src, dst, wr.at[odd, i]).start()
-
-            @pl.when(jnp.logical_not(stays(b)))
-            def _():
-                for i in range(2):
+            for i in range(3):
+                @pl.when(stays(b, i))
+                def _():
+                    src, dst = scatter_parts(b)[i]
+                    pltpu.make_async_copy(src, dst, wr.at[x, i]).start()
+
+                @pl.when(jnp.logical_not(stays(b, i)))
+                def _():
                     scatter_copy(b, i).start()
+
+    def weight_scatter_wait():
         for b in range(2):
-            scatter_copy(b, 2).start()
+            for i in range(3):
+                @pl.when(jnp.logical_not(stays(b, i)))
+                def _():
+                    scatter_copy(b, i).wait_send()
 
     wide = ((0, 384), (384, 256))
 
-    def ring_send(kind, view, d, up):
+    def half_of(d):
+        return lax.div(lax.rem(z + d + 8, 8), 4)
+
+    begins = [
+        {d: half_of(d) == (x_half if part_ == 0 else 1 - x_half) for d in range(-4, 5)} for part_ in range(2)
+    ]
+
+    def ring_send(kind, view, d, up, when=None):
         to = at_z(1) if up else at_z(-1)
         there = d - 1 if up else d + 1
         half = None if abs(there) < 4 else 0 if up else 1
-        put((kind, there), view(d, half), lambda: view(d, half), to)
-
-    def core_send(kind, view, d):
-        put((kind, "core", d), view(d, None), lambda: view(d, None), sibling)
+        put((kind, there), view(d, half), lambda: view(d, half), to, when=when)
+
+    def core_send(kind, view, d, when=None):
+        put((kind, "core", d), view(d, None), lambda: view(d, None), sibling, when=when)
 
     def weight_view(part_, whose):
         cols = pl.ds(*wide[part_])
 
         def view(d, half):
-            there = lax.rem(z + d + 8, 8)
-            index = lax.rem(there, 4) * 2 + lax.div(there, 4)
+            index = lax.rem(z + d + 8, 4) * 2
             if half is None:
-                return weight.at[index, :, whose, :, cols]
-            return weight.at[index, half, whose, :, cols]
+                return weight.at[pl.ds(index, 2), :, whose, :, cols]
+            return weight.at[index + half, :, whose, :, cols]
         return view
 
     def weight_step(part_, number):
         view = weight_view(part_, core)
         kind = ("w", part_)
+        begin = begins[part_]
         if number == 0:
-            for i in range(2):
-                for k, cols in (((0, (0, 256)), (1, (256, 128))), ((2, (384, 256)),))[part_]:
-                    landing = weight.at[z_lo * 2 + z_hi, i, core, :, pl.ds(*cols)]
-                    pltpu.make_async_remote_copy(
-                        src_ref=landing, dst_ref=landing, send_sem=ws.at[0, k], recv_sem=wr.at[i, k],
-                        device_id=sibling, device_id_type=MESH,
-                    ).wait_recv()
-            for up in (True, False):
-                ring_send(kind, view, 0, up)
-            core_send(kind, view, 0)
-        elif number < 5:
-            ring_step(kind, view, number)
+            @pl.when(begin[0])
+            def _():
+                for i in range(4):
+                    for k, cols in (((0, (0, 256)), (1, (256, 128))), ((2, (384, 256)),))[part_]:
+                        landing = weight.at[z_lo * 2 + i // 2, i % 2, core, :, pl.ds(*cols)]
+                        pltpu.make_async_remote_copy(
+                            src_ref=landing, dst_ref=landing, send_sem=ws.at[0, k], recv_sem=wr.at[i, k],
+                            device_id=sibling, device_id_type=MESH,
+                        ).wait_recv()
+                for up in (True, False):
+                    ring_send(kind, view, 0, up, begin[0])
+                core_send(kind, view, 0, begin[0])
+        elif number < 4:
+            for d, up in ((-number, True), (number, False)):
+                @pl.when(begin[d])
+                def _():
+                    got((kind, d), view(d, None))
+                    ring_send(kind, view, d, up, begin[d])
+                    core_send(kind, view, d, begin[d])
+        elif number == 4:
+            @pl.when(begin[4])
+            def _():
+                got((kind, -4), view(-4, 0))
+                got((kind, 4), view(4, 1))
+                core_send(kind, view, 4, begin[4])
         else:
             for d in (0, -1, 1, -2, 2, -3, 3, 4):
-                got((kind, "core", d), weight_view(part_, 1 - core)(d, None))
+                @pl.when(begin[d])
+                def _():
+                    got((kind, "core", d), weight_view(part_, 1 - core)(d, None))
 
     def ring_step(kind, view, number):
         if number < 4:
@@ -335,7 +362,7 @@
             there = lax.rem(x + dx, 4) * 4 + lax.rem(y + dy, 4)
             for k in range(WIN):
                 staged[unit, d, k] = g[list_s[there, 0, k]]
-            dst = arrived.at[x * 4 + y, :, :, pl.ds(unit * TILE, TILE)]
+            dst = arrived.at[unit, x * 4 + y]
 
             @pl.when(d == 0)
             def _():
@@ -352,14 +379,14 @@
         lax.fori_loop(0, 16, one, 0)
 
     def window_wait(unit):
-        dst0 = arrived.at[x * 4 + y, :, :, pl.ds(unit * TILE, TILE)]
+        dst0 = arrived.at[unit, x * 4 + y]
         pltpu.make_async_copy(staged.at[unit, 0], dst0, dr.at[unit, 0]).wait()
 
         def one(d, _):
             dx, dy = lax.div(d, 4), lax.rem(d, 4)
             here = lax.rem(x - dx + 4, 4) * 4 + lax.rem(y - dy + 4, 4)
             copy = pltpu.make_async_remote_copy(
-                src_ref=staged.at[unit, d], dst_ref=arrived.at[here, :, :, pl.ds(unit * TILE, TILE)],
+                src_ref=staged.at[unit, d], dst_ref=arrived.at[unit, here],
                 send_sem=ds.at[unit, d], recv_sem=dr.at[unit, d],
                 device_id=at_xy(dx, dy), device_id_type=MESH,
             )
@@ -445,33 +472,31 @@
     own = table.at[enc]
     put("one", own, lambda: own, sibling)
     put("bias", own_bias, lambda: other_bias, across)
-    vit_step(0, 1)
     weight_step(0, 0)
     weight_step(1, 0)
+    vit_step(0, 1)
+    weight_step(0, 1)
+    weight_step(1, 1)
     vit_step(0, 2)
     got("one", table.at[z_lo * 8 + x * 2 + 1 - core])
     pair = table.at[pl.ds(z_lo * 8 + x * 2, 2)]
     for d in (1, 2, 3):
         put(("pair", d), pair, lambda: pair, at_xy(d, 0))
-    weight_step(0, 1)
-    weight_step(1, 1)
     weight_step(0, 2)
+    weight_step(1, 2)
+    weight_step(0, 3)
+    weight_step(1, 3)
     vit_step(0, 3)
     vit_step(0, 4)
     vit_step(0, 5)
-    weight_step(1, 2)
-    weight_step(0, 3)
-    vit_step(0, 7)
-    weight_step(1, 3)
+    weight_step(0, 4)
+    weight_step(1, 4)
     for d in (1, 2, 3):
         got(("pair", d), table.at[pl.ds(z_lo * 8 + lax.rem(x - d + 4, 4) * 2, 2)])
     eight = table.at[pl.ds(z_lo * 8, 8)]
     for d in (1, 2, 3):
         put(("eight", d), eight, lambda: eight, at_lo(d))
-    weight_step(0, 4)
-    vit_step(0, 6)
-    vit_own(1)
-    weight_step(1, 4)
+    vit_step(0, 7)
     weight_step(0, 5)
     weight_step(1, 5)
     mine.wait()
@@ -482,12 +507,18 @@
     unit_step(1, 0, 0)
     unit_step(0, 0, 1)
     unit_step(1, 0, 1)
+    vit_step(0, 6)
+    vit_own(1)
+    unit_step(0, 0, 2)
+    unit_step(1, 0, 2)
+    unit_step(0, 0, 3)
+    unit_step(1, 0, 3)
     vit_step(0, 8)
     project(1, *a)
     unit_step(0, 1, 0)
     unit_step(1, 1, 0)
-    unit_step(0, 0, 2)
-    unit_step(1, 0, 2)
+    unit_step(0, 0, 4)
+    unit_step(1, 0, 4)
     for d in (1, 2, 3):
         got(("eight", d), table.at[pl.ds(lax.rem(z_lo - d + 4, 4) * 8, 8)])
     own_list()
@@ -512,12 +543,8 @@
         if even:
             project(0, *b)
             project(1, *b)
-        unit_step(0, 0, 3)
-        unit_step(1, 0, 3)
         unit_step(0, 1, 1)
         unit_step(1, 1, 1)
-        unit_step(0, 0, 4)
-        unit_step(1, 0, 4)
         if even:
             unit_step(2, 0, 0)
             unit_step(2, 1, 0)
@@ -531,55 +558,63 @@
             project(0, *b)
             unit_step(2, 0, 0)
         project(0, *c)
-        unit_step(3, 0, 0)
-        unit_step(4, 0, 0)
-        unit_step(0, 1, 3)
-        vit_step(1, 6)
-        unit_step(1, 1, 3)
-        unit_step(0, 1, 4)
-        list_wait()
-        window(0)
-        vit_step(1, 8)
         if even:
-            project(1, *c)
-            unit_step(3, 1, 0)
+            unit_step(2, 0, 1)
+            unit_step(2, 1, 1)
+            vit_step(1, 6)
+            unit_step(0, 1, 3)
+            unit_step(1, 1, 3)
+            unit_step(0, 1, 4)
+            list_wait()
+            window(0)
+            vit_step(1, 8)
+            unit_step(2, 0, 2)
+            unit_step(2, 1, 2)
             unit_step(1, 1, 4)
             window(1)
-            unit_step(2, 0, 1)
-            unit_step(2, 1, 1)
-            small(1)
-            unit_step(2, 0, 2)
-            unit_step(2, 1, 2)
-            unit_step(3, 1, 1)
-            small(2)
+            small(0)
+            project(1, *c)
             unit_step(2, 0, 3)
             unit_step(2, 1, 3)
-            unit_step(3, 1, 2)
-            unit_step(4, 1, 0)
-            small(3)
+            unit_step(3, 1, 0)
+            small(1)
             unit_step(2, 0, 4)
             unit_step(2, 1, 4)
             window(2)
+            small(2)
+            unit_step(3, 1, 1)
+            small(3)
+            unit_step(3, 1, 2)
+            unit_step(4, 1, 0)
             small(4)
         else:
+            unit_step(3, 0, 0)
+            unit_step(4, 0, 0)
+            vit_step(1, 6)
+            unit_step(0, 1, 3)
+            unit_step(1, 1, 3)
+            small(1)
+            unit_step(0, 1, 4)
+            list_wait()
+            window(0)
+            vit_step(1, 8)
             project(1, *b)
             unit_step(2, 1, 0)
             unit_step(1, 1, 4)
+            small(2)
             window(1)
-            small(1)
             project(1, *c)
             unit_step(2, 1, 1)
-            small(2)
+            small(3)
             unit_step(2, 1, 2)
             unit_step(3, 1, 0)
-            small(3)
+            small(4)
             unit_step(2, 1, 3)
-            small(4)
             unit_step(3, 1, 1)
             unit_step(2, 1, 4)
-            unit_step(4, 1, 0)
             window(2)
             unit_step(3, 1, 2)
+            unit_step(4, 1, 0)
         unit_step(3, 1, 3)
         unit_step(4, 1, 1)
         unit_step(3, 1, 4)
@@ -599,31 +634,42 @@
 
     for unit in range(UNITS):
         window_wait(unit)
-    for key in sends:
-        descriptor(key).wait_send()
-    for b in range(2):
-        @pl.when(jnp.logical_not(stays(b)))
-        def _():
-            for i in range(2):
-                scatter_copy(b, i).wait_send()
-        scatter_copy(b, 2).wait_send()
-
-
-def finish(keys, arrived, residual, gain, out):
+    for key, (_, _, when) in sends.items():
+        if when is None:
+            descriptor(key).wait_send()
+        else:
+            @pl.when(when)
+            def _():
+                descriptor(key).wait_send()
+    weight_scatter_wait()
+
+
+def finish(keys, arrived, residual, gain, out, buffer, sem):
     level = pl.program_id(0)
     tokens = residual.shape[1]
-    key = keys[pl.ds(pl.program_id(1), 1), :]
-    hot = jnp.where(lax.broadcasted_iota(I32, (WIN * IMG, tokens), 0) == key, 1.0, 0.0).astype(BF16)
+
+    def fetch(part):
+        units = pl.ds(*((0, 3), (3, 2))[part])
+        return pltpu.make_async_copy(arrived.at[units], buffer.at[units], sem.at[part])
+
+    @pl.when(level == 0)
+    def _():
+        fetch(0).start()
+        fetch(1).start()
+
+    key = jnp.concatenate([keys[0:1, :], keys[1:2, :]], axis=1)
+    hot = jnp.where(lax.broadcasted_iota(I32, (WIN * IMG, tokens), 0) == key, 1.0, 0.0)
+    hot = hot.T.astype(BF16)
 
     def for_level(lvl):
+        fetch(lvl).wait()
         square = jnp.zeros((tokens, TILE), F32)
 
-        def add(start, source, column, width, square):
-            rows = arrived[source, :, :, column:column + width].reshape(WIN * IMG, width)
-            deep = lax.dot_general(
-                hot, rows, (((0,), (0,)), ((), ())),
-                preferred_element_type=F32,
-            )
+        def add(start, source, units, square):
+            width = TILE * len(units)
+            rows = [buffer[unit, source].reshape(WIN * IMG, TILE) for unit in units]
+            rows = jnp.concatenate(rows, axis=1) if len(units) > 1 else rows[0]
+            deep = jnp.dot(hot, rows, preferred_element_type=F32)
             total = (residual[0, :, start:start + width].astype(F32) + deep).astype(BF16)
             out[0, :, start:start + width] = total
             total = total.astype(F32)
@@ -637,11 +683,11 @@
             base = ((sx // 2) * 4 + sy) * 640
             other = ((1 - sx // 2) * 4 + sy) * 640
             if lvl == 0:
-                square = add(base + 384 * (sx % 2), source, 0, 256, square)
+                square = add(base + 384 * (sx % 2), source, (0, 1), square)
             else:
-                square = add(other + 384 * (sx % 2), source, 384, 256, square)
+                square = add(other + 384 * (sx % 2), source, (3, 4), square)
             if sx % 2 == lvl:
-                square = add(base + 256, source, 256, 128, square)
+                square = add(base + 256, source, (2,), square)
         mean = jnp.sum(square, axis=1, keepdims=True) * (1.0 / 5120)
         scale = lax.rsqrt(mean + 1e-06)
         for start in range(0, 5120, 512):
@@ -668,7 +714,7 @@
         exchange,
         name="exchange",
         out_shape=(
-            jax.ShapeDtypeStruct((16, WIN, IMG, UNITS * TILE), BF16),
+            jax.ShapeDtypeStruct((UNITS, 16, WIN, IMG, TILE), BF16),
             jax.ShapeDtypeStruct((8, 128), I32),
         ),
         in_specs=[any_, any_, vmem, pl.BlockSpec(memory_space=pltpu.SMEM), vmem],
@@ -691,7 +737,7 @@
             pltpu.SemaphoreType.DMA((SENDS,)),
             pltpu.SemaphoreType.DMA((2,)),
             pltpu.SemaphoreType.DMA((2, 3)),
-            pltpu.SemaphoreType.DMA((2, 3)),
+            pltpu.SemaphoreType.DMA((4, 3)),
             pltpu.SemaphoreType.DMA((16,)),
             pltpu.SemaphoreType.DMA((16,)),
             pltpu.SemaphoreType.DMA((UNITS, 16)),
@@ -708,15 +754,19 @@
     return pl.pallas_call(
         finish,
         name="finish",
-        grid=(2, 2),
+        grid=(2,),
         out_shape=jax.ShapeDtypeStruct(residual.shape, BF16),
         in_specs=[
-            pl.BlockSpec((8, 128), lambda i, j: (0, 0)),
-            pl.BlockSpec((16, WIN, IMG, UNITS * TILE), lambda i, j: (0, 0, 0, 0)),
-            pl.BlockSpec((1, count // 2, 5120), lambda i, j: (i, j, 0)),
-            pl.BlockSpec((2, 5120), lambda i, j: (0, 0)),
+            pl.BlockSpec((8, 128), lambda i: (0, 0)),
+            any_,
+            pl.BlockSpec((1, count, 5120), lambda i: (i, 0, 0)),
+            pl.BlockSpec((2, 5120), lambda i: (0, 0)),
         ],
-        out_specs=pl.BlockSpec((1, count // 2, 5120), lambda i, j: (i, j, 0)),
+        out_specs=pl.BlockSpec((1, count, 5120), lambda i: (i, 0, 0)),
+        scratch_shapes=[
+            pltpu.VMEM((UNITS, 16, WIN, IMG, TILE), BF16),
+            pltpu.SemaphoreType.DMA((2,)),
+        ],
         compiler_params=pltpu.CompilerParams(vmem_limit_bytes=60 << 20),
     )(keys, arrived, residual, norm_gain)
 

time: 206 us -> 200 us (0.971)
  Pallas kernels: 204 us -> 197 us
    pallas_call x1, Pallas kernels: 193 us -> 186 us  [per_device(): pl.pallas_call(exchange, name='exchange', out_shape=(jax.ShapeDtypeStruct...]
where the time goes in v3:
time: 200 us; the launch traced here: 197 us
  Pallas kernels  197 us (98%)
    pallas_call x1, Pallas kernels, per_device(): pl.pallas_call(exchange, name='exchange', out_shape=(jax.ShapeDtypeStruct...  186 us
    pallas_call x1, Pallas kernels, per_device(): pl.pallas_call(finish, name='finish', grid=(2,), out_shape=jax.ShapeDtype...  10.3 us

profile of v3, /device:TPU:32, one launch (start us, length us, event | category | flops | bytes accessed | tf_op | source)
XLA Modules:
  0.0 196.9 jit_solution(8321700428164212765)
XLA Ops:
  0.0 186.4 %exchange.1 = (bf16[5,16,17,16,128]{4,3,2,1,0:T(8,128)(2,1)}, s32[8,128]{1,0:T(8,128)}) custom-call(bf16[112,4608]{1,0:T(8,128)(2,1)} %bitcast.2, bf16[2,144,640]{2,1,0:T(8,128)(2,1)} %w.1, bf16[2,640]{1,0:T(2,128)(2,1)} %bias.1, s32[28]{0:T(128)} %images.1, s32[16,128]{1,0:T(8,128)} %bitcast.3), custom_call_target="tpu_custom_call" | custom-call | flops 5284823040 | bytes 8388608 | tf_op jit(solution)/shard_map/exchange/pallas_call | solution.py:713
  186.5 10.3 %finish.1 = bf16[2,256,5120]{2,1,0:T(8,128)(2,1)} custom-call(s32[8,128]{1,0:T(8,128)} %get-tuple-element.7.keys, bf16[5,16,17,16,128]{4,3,2,1,0:T(8,128)(2,1)} %get-tuple-element.8.arrived, bf16[2,256,5120]{2,1,0:T(8,128)(2,1)} %residual.1, bf16[2,5120]{1,0:T(2,128)(2,1)} %gain.1), custom_call_target="tpu_custom_call" | custom-call | tf_op jit(solution)/shard_map/finish/pallas_call | solution.py:754

commit v4 on v3

--- a/solution.py
+++ b/solution.py
@@ -357,7 +357,8 @@
     def window_send(unit):
         g = gathered[unit]
 
-        def one(d, _):
+        def one(i, _):
+            d = lax.rem(i * 7 + 10, 16)
             dx, dy = lax.div(d, 4), lax.rem(d, 4)
             there = lax.rem(x + dx, 4) * 4 + lax.rem(y + dy, 4)
             for k in range(WIN):
@@ -644,25 +645,27 @@
     weight_scatter_wait()
 
 
-def finish(keys, arrived, residual, gain, out, buffer, sem):
-    level = pl.program_id(0)
+def finish(keys, arrived, residual, gain, out, buffer, stream, result, sem, out_sem):
     tokens = residual.shape[1]
-
-    def fetch(part):
-        units = pl.ds(*((0, 3), (3, 2))[part])
-        return pltpu.make_async_copy(arrived.at[units], buffer.at[units], sem.at[part])
-
-    @pl.when(level == 0)
-    def _():
-        fetch(0).start()
-        fetch(1).start()
+    half = tokens // 2
+    fetches = []
+    for lvl in range(2):
+        units = pl.ds(*((0, 3), (3, 2))[lvl])
+        fetches.append((
+            pltpu.make_async_copy(residual.at[lvl], stream.at[lvl], sem.at[lvl, 0]),
+            pltpu.make_async_copy(arrived.at[units], buffer.at[units], sem.at[lvl, 1]),
+        ))
+    for pair in fetches:
+        for copy in pair:
+            copy.start()
 
     key = jnp.concatenate([keys[0:1, :], keys[1:2, :]], axis=1)
     hot = jnp.where(lax.broadcasted_iota(I32, (WIN * IMG, tokens), 0) == key, 1.0, 0.0)
     hot = hot.T.astype(BF16)
-
-    def for_level(lvl):
-        fetch(lvl).wait()
+    stores = []
+    for lvl in range(2):
+        for copy in fetches[lvl]:
+            copy.wait()
         square = jnp.zeros((tokens, TILE), F32)
 
         def add(start, source, units, square):
@@ -670,8 +673,8 @@
             rows = [buffer[unit, source].reshape(WIN * IMG, TILE) for unit in units]
             rows = jnp.concatenate(rows, axis=1) if len(units) > 1 else rows[0]
             deep = jnp.dot(hot, rows, preferred_element_type=F32)
-            total = (residual[0, :, start:start + width].astype(F32) + deep).astype(BF16)
-            out[0, :, start:start + width] = total
+            total = (stream[lvl, :, start:start + width].astype(F32) + deep).astype(BF16)
+            result[lvl, :, start:start + width] = total
             total = total.astype(F32)
             for i in range(0, width, TILE):
                 piece = total[:, i:i + TILE]
@@ -690,18 +693,20 @@
                 square = add(base + 256, source, (2,), square)
         mean = jnp.sum(square, axis=1, keepdims=True) * (1.0 / 5120)
         scale = lax.rsqrt(mean + 1e-06)
-        for start in range(0, 5120, 512):
-            cols = slice(start, start + 512)
-            values = out[0, :, cols].astype(F32)
-            out[0, :, cols] = (values * scale * gain[lvl:lvl + 1, cols].astype(F32)).astype(BF16)
-
-    @pl.when(level == 0)
-    def _():
-        for_level(0)
-
-    @pl.when(level == 1)
-    def _():
-        for_level(1)
+        for part in range(2):
+            rows = slice(part * half, (part + 1) * half)
+            for start in range(0, 5120, 512):
+                cols = slice(start, start + 512)
+                values = result[lvl, rows, cols].astype(F32)
+                result[lvl, rows, cols] = (
+                    values * scale[rows] * gain[lvl:lvl + 1, cols].astype(F32)
+                ).astype(BF16)
+            place_ = pl.ds(part * half, half)
+            copy = pltpu.make_async_copy(result.at[lvl, place_], out.at[lvl, place_], out_sem.at[lvl, part])
+            copy.start()
+            stores.append(copy)
+    for copy in stores:
+        copy.wait()
 
 
 def per_device(
@@ -754,18 +759,15 @@
     return pl.pallas_call(
         finish,
         name="finish",
-        grid=(2,),
         out_shape=jax.ShapeDtypeStruct(residual.shape, BF16),
-        in_specs=[
-            pl.BlockSpec((8, 128), lambda i: (0, 0)),
-            any_,
-            pl.BlockSpec((1, count, 5120), lambda i: (i, 0, 0)),
-            pl.BlockSpec((2, 5120), lambda i: (0, 0)),
-        ],
-        out_specs=pl.BlockSpec((1, count, 5120), lambda i: (i, 0, 0)),
+        in_specs=[vmem, any_, any_, vmem],
+        out_specs=any_,
         scratch_shapes=[
             pltpu.VMEM((UNITS, 16, WIN, IMG, TILE), BF16),
-            pltpu.SemaphoreType.DMA((2,)),
+            pltpu.VMEM((2, count, 5120), BF16),
+            pltpu.VMEM((2, count, 5120), BF16),
+            pltpu.SemaphoreType.DMA((2, 2)),
+            pltpu.SemaphoreType.DMA((2, 2)),
         ],
         compiler_params=pltpu.CompilerParams(vmem_limit_bytes=60 << 20),
     )(keys, arrived, residual, norm_gain)

time: 200 us -> 198 us (0.990)
  Pallas kernels: 197 us -> 195 us
where the time goes in v4:
time: 198 us; the launch traced here: 195 us
  Pallas kernels  195 us (98%)
    pallas_call x1, Pallas kernels, per_device(): pl.pallas_call(exchange, name='exchange', out_shape=(jax.ShapeDtypeStruct...  185 us
    pallas_call x1, Pallas kernels, per_device(): pl.pallas_call(finish, name='finish', out_shape=jax.ShapeDtypeStruct(resi...  9.81 us

profile of v4, /device:TPU:32, one launch (start us, length us, event | category | flops | bytes accessed | tf_op | source)
XLA Modules:
  0.0 194.9 jit_solution(2261632064224530973)
XLA Ops:
  0.0 185.0 %exchange.1 = (bf16[5,16,17,16,128]{4,3,2,1,0:T(8,128)(2,1)}, s32[8,128]{1,0:T(8,128)}) custom-call(bf16[112,4608]{1,0:T(8,128)(2,1)} %bitcast.2, bf16[2,144,640]{2,1,0:T(8,128)(2,1)} %w.1, bf16[2,640]{1,0:T(2,128)(2,1)} %bias.1, s32[28]{0:T(128)} %images.1, s32[16,128]{1,0:T(8,128)} %bitcast.3), custom_call_target="tpu_custom_call" | custom-call | flops 5284823040 | bytes 8388608 | tf_op jit(solution)/shard_map/exchange/pallas_call | solution.py:718
  185.0 9.8 %finish.1 = bf16[2,256,5120]{2,1,0:T(8,128)(2,1)} custom-call(s32[8,128]{1,0:T(8,128)} %get-tuple-element.7.keys, bf16[5,16,17,16,128]{4,3,2,1,0:T(8,128)(2,1)} %get-tuple-element.8.arrived, bf16[2,256,5120]{2,1,0:T(8,128)(2,1)} %residual.1, bf16[2,5120]{1,0:T(2,128)(2,1)} %gain.1), custom_call_target="tpu_custom_call" | custom-call | tf_op jit(solution)/shard_map/finish/pallas_call | solution.py:759
